TPU v7x, 256 devices: a whole 4x4x8 slice. The times are simulated.
256 devices in a mesh: ops: 16 (over z, core), sec: 16 (over y, x).
Axes of the slice: x: 4, y: 4, z: 8, core: 2. Of those that a mesh axis runs over, the one named last changes fastest.
Arguments:
- wavefunction: float32 [64, 256, 256], P('sec', 'ops'), may hold values from -64 to 64
- left_operators: float32 [64, 64, 256, 256], P('ops', 'sec'), may hold values from -8 to 8
- right_operators: float32 [64, 64, 256, 256], P('ops', 'sec'), may hold values from -8 to 8
- preconditioner: float32 [64, 256, 256], P('sec', 'ops'), may hold values from 1 to 10
- charges: int32 [64], P('ops'), may hold values from -1 to 1
- coupling: int32 [64, 64], P('ops', 'sec'), may hold values from 0 to 1
Outputs:
- correction: float32 [64, 256, 256], P('sec', 'ops')
- image_new: float32 [64, 256, 256], P('sec', 'ops')
All inputs are finite; a program needn't handle non-finite values.
Results may differ from a plain program's by a relative error of at most 0.0007.
Values sent between devices are 32-bit elements; how exact they have to be, the bound alone decides.
No kernel may reach another device: no remote copies, remote signals or barrier semaphores. Data moves between devices by JAX's collectives and lax.ppermute only.
A program may use at most 64 MiB of HBM per device.

v0:
```python
import jax
import jax.numpy as jnp
from jax import lax
from jax.sharding import PartitionSpec as P

PRECISE = lax.Precision.HIGHEST
EPSILON = 1e-06


def padded(block, sides, width):
    for axis, dim in sides:
        count = lax.axis_size(axis)
        forward = [(i, i + 1) for i in range(count - 1)]
        backward = [(target, source) for source, target in forward]
        low = lax.ppermute(
            lax.slice_in_dim(block, block.shape[dim] - width, None, axis=dim), axis, forward
        )
        high = lax.ppermute(lax.slice_in_dim(block, 0, width, axis=dim), axis, backward)
        block = jnp.concatenate([low, block, high], axis=dim)
    return block


def block_product(left_block, vector_block, right_block):
    left_applied = jnp.dot(
        left_block, vector_block, precision=PRECISE, preferred_element_type=jnp.float32
    )
    return lax.dot_general(
        left_applied,
        right_block,
        (((1,), (1,)), ((), ())),
        precision=PRECISE,
        preferred_element_type=jnp.float32,
    )


def local_images(blocks, left_operators, right_operators, charges, coupling):
    term_count = left_operators.shape[0]
    pair_count = left_operators.shape[1]
    block_order = blocks.shape[1]
    starting = jnp.zeros((pair_count + 2, block_order, block_order), jnp.float32)

    def visit_item(position, buffer):
        term_index = position // pair_count
        pair_index = position % pair_count

        def contribute(current):
            product = block_product(
                left_operators[term_index, pair_index],
                blocks[pair_index],
                right_operators[term_index, pair_index],
            )
            target = pair_index + 1 + charges[term_index]
            existing = lax.dynamic_slice_in_dim(current, target, 1, 0)
            return lax.dynamic_update_slice_in_dim(current, existing + product[None], target, 0)

        return lax.cond(
            coupling[term_index, pair_index] > 0, contribute, lambda current: current, buffer
        )

    return lax.fori_loop(0, term_count * pair_count, visit_item, starting)


def fold_ghosts(extended):
    inner_part = extended[2:-2]
    inner_part = inner_part.at[0].add(extended[0])
    inner_part = inner_part.at[-1].add(extended[-1])
    return inner_part


def apply_operator(slab, left_operators, right_operators, charges, coupling):
    blocks = lax.all_gather(slab, "ops", axis=1, tiled=True)
    buffer = local_images(blocks, left_operators, right_operators, charges, coupling)
    extended = padded(buffer, (("sec", 0),), 1)
    return lax.psum_scatter(fold_ghosts(extended), "ops", scatter_dimension=1, tiled=True)


def on_device(wavefunction, left_operators, right_operators, preconditioner, charges, coupling):
    entries = wavefunction.size * lax.axis_size("ops") * lax.axis_size("sec")
    image_psi = apply_operator(wavefunction, left_operators, right_operators, charges, coupling)
    psi_norm, correlation = lax.psum(
        (jnp.sum(wavefunction * wavefunction), jnp.sum(wavefunction * image_psi)), ("ops", "sec")
    )
    rayleigh = correlation / psi_norm
    scaled = (image_psi - rayleigh * wavefunction) / preconditioner
    projection = lax.psum(jnp.sum(wavefunction * scaled), ("ops", "sec"))
    orthogonal = scaled - projection / psi_norm * wavefunction
    squares = lax.psum(jnp.sum(orthogonal * orthogonal), ("ops", "sec"))
    correction = orthogonal / jnp.sqrt(squares / entries + EPSILON)
    image_new = apply_operator(correction, left_operators, right_operators, charges, coupling)
    return (correction, image_new)


def solution(mesh):
    placed = (
        P("sec", "ops", None),
        P("ops", "sec", None, None),
        P("ops", "sec", None, None),
        P("sec", "ops", None),
        P("ops"),
        P("ops", "sec"),
    )
    return jax.shard_map(
        on_device,
        mesh=mesh,
        in_specs=placed,
        out_specs=(P("sec", "ops", None), P("sec", "ops", None)),
        check_vma=False,
    )
```

profile of v0, /device:TPU:1, one launch (start us, length us, event | category | flops | bytes accessed | tf_op | source)
XLA Modules:
  0.0 624.9 jit_solution(9722210980238410861)
XLA Ops:
  8.0 44.8 %all-gather.3.cloned.1.call-done = f32[4,256,256]{2,1,0:T(8,128)} async-done(((f32[4,16,256]{2,1,0:T(8,128)}), f32[4,256,256]{2,1,0:T(8,128)}) %all-gather.3.cloned.1.call-update) | async-done | bytes 1048592 | tf_op jit(solution)/shard_map/all_gather | solution.py:71
  52.9 57.7 %while.40 = (s32[]{:T(128)}, f32[6,256,256]{2,1,0:T(8,128)S(1)}, s32[4,4]{1,0:T(4,128)S(1)}, s32[4]{0:T(128)S(1)}, f32[4,4,256,256]{3,2,1,0:T(8,128)}, /*index=5...) while((s32[]{:T(128)}, f32[6,256,256]{2,1,0:T(8,128)S(1)}, ...), condition=%wide.region_3.4_spmd, body=%wide.region_0.3_spmd.sunk | while | flops 402718752 | bytes 1837108 | solution.py:60
  56.8 4.1 conditional.4
  58.1 1.4 fusion.3
  59.5 1.4 fusion.1
  62.2 4.1 conditional.4
  63.5 1.4 fusion.3
  64.9 1.4 fusion.1
  67.6 4.1 conditional.4
  68.9 1.4 fusion.3
  70.3 1.4 fusion.1
  75.6 4.1 conditional.4
  76.9 1.4 fusion.3
  81.0 4.1 conditional.4
  82.3 1.4 fusion.3
  83.7 1.4 fusion.1
  89.0 4.1 conditional.4
  90.3 1.4 fusion.3
  91.7 1.4 fusion.1
  94.4 4.1 conditional.4
  95.7 1.4 fusion.3
  97.1 1.4 fusion.1
  99.8 4.1 conditional.4
  101.1 1.4 fusion.3
  102.5 1.4 fusion.1
  106.5 4.1 conditional.4
  107.8 1.4 fusion.3
  113.4 1.9 collective-permute-done
  115.3 5.3 collective-permute-done.1
  121.7 78.7 %reduce-scatter.3.cloned.1.call-done = f32[4,16,256]{2,1,0:T(8,128)} async-done(((f32[4,256,256]{2,1,0:T(8,128)}), f32[4,16,256]{2,1,0:T(8,128)}) %reduce-scatter.3.cloned.1.call-update) | async-done | bytes 65552 | tf_op jit(solution)/shard_map/reduce_scatter | solution.py:74
  200.4 1.5 multiply_reduce_fusion.2
  201.8 79.7 %all-reduce = (f32[]{:T(128)}, f32[]{:T(128)}) all-reduce(f32[]{:T(128)} %get-tuple-element.475, f32[]{:T(128)} %get-tuple-element.474), channel_id=1, replica_groups=mesh['ops'=16,'sec'=16] {'ops','sec'}, use_global_device_ids=true, to_apply=%region_6.7 | all-reduce | flops 2 | bytes 16 | tf_op jit(solution)/shard_map/psum | solution.py:80
  282.9 1.5 multiply_reduce_fusion.1
  284.3 72.6 %psum.30 = f32[]{:T(128)} all-reduce(f32[]{:T(128)} %multiply_reduce_fusion.1), channel_id=1, replica_groups=mesh['ops'=16,'sec'=16] {'ops','sec'}, use_global_device_ids=true, to_apply=%region_10.11 | all-reduce | flops 1 | bytes 8 | tf_op jit(solution)/shard_map/psum | solution.py:85
  358.3 1.5 multiply_reduce_fusion
  359.8 73.5 %psum.31 = f32[]{:T(128)} all-reduce(f32[]{:T(128)} %multiply_reduce_fusion), channel_id=1, replica_groups=mesh['ops'=16,'sec'=16] {'ops','sec'}, use_global_device_ids=true, to_apply=%region_12.13 | all-reduce | flops 1 | bytes 8 | tf_op jit(solution)/shard_map/psum | solution.py:87
  434.0 1.5 broadcast_divide_fusion
  435.5 35.7 %all-gather.5.cloned.1.call-done = f32[4,256,256]{2,1,0:T(8,128)} async-done(((f32[4,16,256]{2,1,0:T(8,128)}), f32[4,256,256]{2,1,0:T(8,128)}) %all-gather.5.cloned.1.call-update) | async-done | bytes 1048592 | tf_op jit(solution)/shard_map/all_gather | solution.py:71
  471.3 57.6 %while.41 = (s32[]{:T(128)}, f32[6,256,256]{2,1,0:T(8,128)S(1)}, s32[4,4]{1,0:T(4,128)S(1)}, s32[4]{0:T(128)S(1)}, f32[4,4,256,256]{3,2,1,0:T(8,128)}, /*index=5...) while((s32[]{:T(128)}, f32[6,256,256]{2,1,0:T(8,128)S(1)}, ...), condition=%wide.region_16.17_spmd, body=%wide.region_13.16_spmd.sunk | while | flops 402718752 | bytes 1837108 | solution.py:60
  475.3 4.1 conditional.5
  476.5 1.4 fusion.14
  480.7 4.0 conditional.5
  481.9 1.4 fusion.14
  486.0 4.1 conditional.5
  487.3 1.4 fusion.14
  488.7 1.4 fusion.12
  494.1 4.1 conditional.5
  495.3 1.4 fusion.14
  499.4 4.1 conditional.5
  500.7 1.4 fusion.14
  502.1 1.4 fusion.12
  507.4 4.1 conditional.5
  508.7 1.4 fusion.14
  512.8 4.1 conditional.5
  514.1 1.4 fusion.14
  515.5 1.4 fusion.12
  518.2 4.1 conditional.5
  519.4 1.4 fusion.14
  524.9 4.1 conditional.5
  526.1 1.4 fusion.14
  527.6 1.4 fusion.12
  531.7 1.9 collective-permute-done.2
  533.6 5.3 collective-permute-done.3
  540.0 78.4 %reduce-scatter.5.cloned.1.call-done = f32[4,16,256]{2,1,0:T(8,128)} async-done(((f32[4,256,256]{2,1,0:T(8,128)}), f32[4,16,256]{2,1,0:T(8,128)}) %reduce-scatter.5.cloned.1.call-update) | async-done | bytes 65552 | tf_op jit(solution)/shard_map/reduce_scatter | solution.py:74
  (105 shorter events, 49.9 us)
Async XLA Ops:
  7.2 45.7 %copy-start.4 = (s32[4,4]{1,0:T(4,128)S(1)}, s32[4,4]{1,0:T(4,128)}, u32[]{:S(2)}) copy-start(s32[4,4]{1,0:T(4,128)} %param.27) | copy-start | bytes 196
  7.2 45.7 %copy-start.5 = (s32[4]{0:T(128)S(1)}, s32[4]{0:T(128)}, u32[]{:S(2)}) copy-start(s32[4]{0:T(128)} %param.26) | copy-start | bytes 52
  7.2 45.6 %all-gather.3.cloned.1.call-start = ((), (), s32[]{:S(2)}) async-start(), calls=%async_computation.2 | async-start | bytes 1114112 | tf_op jit(solution)/shard_map/all_gather | solution.py:71
  7.9 192.5 %reduce-scatter.3.cloned.1.call-start = ((), (), s32[]{:S(2)}) async-start(), calls=%async_computation.3 | async-start | bytes 1114112 | tf_op jit(solution)/shard_map/reduce_scatter | solution.py:74
  110.6 4.6 collective-permute-start
  111.9 8.6 %collective-permute-start.1 = (f32[1,256,256]{2,1,0:T(8,128)S(1)}, f32[1,256,256]{2,1,0:T(8,128)S(1)}, u32[]{:S(2)}, u32[]{:S(2)}) collective-permute-start(f32[1,256,256]{2,1,0:T(8,128)S(1)} %get-tuple-element.508), channel_id=1, source_target_pairs={{1,0},{2,1},{3,2},{4,3},{5,4},{6,5},{7,6},{8,7},{9,8},{10,9},{11,1... | collective-permute-start | bytes 786440 | tf_op jit(solution)/shard_map/ppermute | solution.py:18
  113.3 87.0 %copy-start.2 = (f32[4,16,256]{2,1,0:T(8,128)S(1)}, f32[4,16,256]{2,1,0:T(8,128)}, u32[]{:S(2)}) copy-start(f32[4,16,256]{2,1,0:T(8,128)} %param.22) | copy-start | bytes 196612
  113.3 169.5 %copy-start.3 = (f32[4,16,256]{2,1,0:T(8,128)S(1)}, f32[4,16,256]{2,1,0:T(8,128)}, u32[]{:S(2)}) copy-start(f32[4,16,256]{2,1,0:T(8,128)} %param.25) | copy-start | bytes 196612
  120.6 1.0 copy-start
  121.6 349.5 %all-gather.5.cloned.1.call-start = ((), (), s32[]{:S(2)}) async-start(), calls=%async_computation.4 | async-start | bytes 1114112 | tf_op jit(solution)/shard_map/all_gather | solution.py:71
  435.5 182.9 %reduce-scatter.5.cloned.1.call-start = ((), (), s32[]{:S(2)}) async-start(), calls=%async_computation.5 | async-start | bytes 1114112 | tf_op jit(solution)/shard_map/reduce_scatter | solution.py:74
  529.0 4.6 collective-permute-start.2
  530.3 8.6 %collective-permute-start.3 = (f32[1,256,256]{2,1,0:T(8,128)S(1)}, f32[1,256,256]{2,1,0:T(8,128)S(1)}, u32[]{:S(2)}, u32[]{:S(2)}) collective-permute-start(f32[1,256,256]{2,1,0:T(8,128)S(1)} %get-tuple-element.506), channel_id=1, source_target_pairs={{1,0},{2,1},{3,2},{4,3},{5,4},{6,5},{7,6},{8,7},{9,8},{10,9},{11,1... | collective-permute-start | bytes 786440 | tf_op jit(solution)/shard_map/ppermute | solution.py:18
  539.0 1.0 copy-start.1
Sparse Core Ops, SparseCore 0:
  9.9 42.8 all-gather.2
  121.8 78.5 reduce-scatter.2
  435.6 35.5 all-gather.4
  540.1 78.2 reduce-scatter.4
where the time goes:
time: 630 us; the launch traced here: 625 us
  waiting for transfers between devices  253 us (40%)
  blocking collectives  226 us (36%)
  matrix products  50.1 us (8%)
  local copies, waits for them, and re-layouts  33.8 us (5%)
  loops' own time  33.8 us (5%)
  between operations  17.3 us (3%)
    reduce_scatter x2, waiting for transfers between devices, apply_operator(): lax.psum_scatter(fold_ghosts(extended), 'ops', scatter_dimension=1, tiled...  157 us
    all_gather x2, waiting for transfers between devices, apply_operator(): blocks = lax.all_gather(slab, 'ops', axis=1, tiled=True)  80.5 us
    psum x1, blocking collectives, on_device(): lax.psum((jnp.sum(wavefunction * wavefunction), jnp.sum(wavefunction * im...  79.7 us
    psum x1, blocking collectives, on_device(): squares = lax.psum(jnp.sum(orthogonal * orthogonal), ('ops', 'sec'))  73.5 us
    psum x1, blocking collectives, on_device(): projection = lax.psum(jnp.sum(wavefunction * scaled), ('ops', 'sec'))  72.6 us
    dot_general x18, matrix products, block_product(): jnp.dot(left_block, vector_block, precision=PRECISE, preferred_element_ty...  25.4 us
    dot_general x18, matrix products, block_product(): lax.dot_general(left_applied, right_block, (((1,), (1,)), ((), ())), prec...  24.6 us
    another operation x2, loops' own time, local_images(): return lax.fori_loop(0, term_count * pair_count, visit_item, starting)  21.6 us
  transfers between devices with their start and end apart: 8, of which 8 were waited for; matrix products, arithmetic and copies ran while one was open for 0% of the time, Pallas kernels for 0%

commit v1 on v0

v1 whole, which is shorter than its diff:
```python
import functools

import jax
import jax.numpy as jnp
from jax import lax
from jax.experimental import pallas as pl
from jax.experimental.pallas import tpu as pltpu
from jax.sharding import PartitionSpec as P

EPSILON = 1e-06
F32 = jnp.float32
BF16 = jnp.bfloat16
BLK = 256
ROWS = 16
NZ = 8
NT = (((1,), (1,)), ((), ()))
NN = (((1,), (0,)), ((), ()))


def split(x):
    high = x.astype(BF16)
    return high, (x - high.astype(F32)).astype(BF16)


def product(a, b, dims):
    (ah, al), (bh, bl) = split(a), b
    dot = functools.partial(lax.dot_general, dimension_numbers=dims, preferred_element_type=F32)
    return dot(ah, bh) + (dot(ah, bl) + dot(al, bh))


def items_kernel(first, stride, has_start, core, charges, coupling, left, right, own, other, *rest):
    if has_start:
        start, *rest = rest
    *outs, acc, vector_high, vector_low = rest
    step, term = pl.program_id(0), pl.program_id(1)
    pair = first + stride * step

    @pl.when((step == 0) & (term == 0))
    def _():
        if has_start:
            acc[1:5] = start[...]
        else:
            acc[...] = jnp.zeros_like(acc)

    @pl.when(term == 0)
    def _():
        rows = pl.ds(pl.multiple_of(pair * ROWS, ROWS), ROWS)
        for z in range(NZ):
            a, b = own[z, rows, :], other[z, rows, :]
            for half, block in enumerate((jnp.where(core[0] == 0, a, b), jnp.where(core[0] == 0, b, a))):
                place = slice((2 * z + half) * ROWS, (2 * z + half + 1) * ROWS)
                vector_high[place, :], vector_low[place, :] = split(block)

    @pl.when(coupling[term, pair] > 0)
    def _():
        applied = product(left[0, 0], (vector_high[...], vector_low[...]), NN)
        block = product(applied, split(right[0, 0]), NT)
        target = pair + 1 + charges[term]
        acc[target] += block

    @pl.when((step == pl.num_programs(0) - 1) & (term == pl.num_programs(1) - 1))
    def _():
        outs[0][...] = acc[1:5]
        if len(outs) > 1:
            outs[1][...] = acc[0]
            outs[2][...] = acc[5]


def items(first, stride, core, charges, coupling, left, right, own, other, start=None):
    block = pl.BlockSpec((1, 1, BLK, BLK), lambda i, k: (k, first + stride * i, 0, 0))
    smem = pl.BlockSpec(memory_space=pltpu.SMEM)
    vmem = pl.BlockSpec(memory_space=pltpu.VMEM)
    inner = jax.ShapeDtypeStruct((4, BLK, BLK), F32)
    edge = jax.ShapeDtypeStruct((BLK, BLK), F32)
    outs = (inner, edge, edge) if start is None else (inner,)
    extra = () if start is None else (start,)
    return pl.pallas_call(
        functools.partial(items_kernel, first, stride, start is not None),
        grid=(2, 4),
        in_specs=[smem, smem, smem, block, block, vmem, vmem] + [vmem] * len(extra),
        out_specs=[vmem] * len(outs),
        out_shape=outs,
        scratch_shapes=[
            pltpu.VMEM((6, BLK, BLK), F32),
            pltpu.VMEM((BLK, BLK), BF16),
            pltpu.VMEM((BLK, BLK), BF16),
        ],
        compiler_params=pltpu.CompilerParams(vmem_limit_bytes=32 * 1024 * 1024),
        cost_estimate=pl.CostEstimate(flops=8 * 6 * 2 * BLK**3, bytes_accessed=8 * 2**19, transcendentals=0),
    )(core, charges, coupling, left, right, own, other, *extra)


def arrange_kernel(core, edges, inner, low, high, own, other, mine, theirs):
    from_low = edges[0] > 0
    from_high = edges[1] > 0
    dots = jnp.zeros((8, BLK), F32)
    norms = jnp.zeros((8, BLK), F32)
    for pair in range(4):
        for z in range(NZ):
            pieces = []
            for half in range(2):
                rows = slice((2 * z + half) * ROWS, (2 * z + half + 1) * ROWS)
                piece = inner[pair, rows, :]
                if pair == 0:
                    piece = piece + jnp.where(from_low, low[rows, :], 0.0)
                if pair == 3:
                    piece = piece + jnp.where(from_high, high[rows, :], 0.0)
                pieces.append(piece)
            place = slice(pair * ROWS, (pair + 1) * ROWS)
            a = jnp.where(core[0] == 0, pieces[0], pieces[1])
            b = jnp.where(core[0] == 0, pieces[1], pieces[0])
            mine[z, place, :] = a
            theirs[z, place, :] = b
            va, vb = own[z, place, :], other[z, place, :]
            d = a * va + b * vb
            n = va * va + vb * vb
            dots += d[:8] + d[8:]
            norms += n[:8] + n[8:]
    row = lax.broadcasted_iota(jnp.int32, (8, BLK), 0)
    sums = jnp.where(row == 0, jnp.sum(dots), 0.0) + jnp.where(row == 1, jnp.sum(norms) * (1.0 / 16), 0.0)
    for z in range(NZ):
        mine[z, 64:72, :] = sums
        theirs[z, 64:72, :] = sums


def arrange(core, edges, inner, low, high, own, other):
    smem = pl.BlockSpec(memory_space=pltpu.SMEM)
    vmem = pl.BlockSpec(memory_space=pltpu.VMEM)
    half = jax.ShapeDtypeStruct((NZ, 72, BLK), F32)
    return pl.pallas_call(
        arrange_kernel,
        in_specs=[smem, smem] + [vmem] * 5,
        out_specs=[vmem, vmem],
        out_shape=(half, half),
        compiler_params=pltpu.CompilerParams(vmem_limit_bytes=32 * 1024 * 1024),
    )(core, edges, inner, low, high, own, other)


SWAP = [(i, i ^ 1) for i in range(16)]
SAME_CORE = [[2 * z + c for z in range(NZ)] for c in range(2)]
UP = [(i, (i + 1) % 16) for i in range(16)]
DOWN = [(i, (i - 1) % 16) for i in range(16)]


def exchange(parts):
    return lax.all_to_all(parts, "ops", 0, 0, axis_index_groups=SAME_CORE)


def gather(slab):
    own = exchange(jnp.broadcast_to(slab[None], (NZ, *slab.shape)))
    return own, lax.ppermute(own, "ops", SWAP)


def image(own, other, core, edges, left, right, charges, coupling):
    inner, low, high = items(0, 3, core, charges, coupling, left, right, own, other)
    from_high = lax.ppermute(low, "sec", DOWN)
    from_low = lax.ppermute(high, "sec", UP)
    inner = items(1, 1, core, charges, coupling, left, right, own, other, inner)[0]
    mine, theirs = arrange(core, edges, inner, from_low, from_high, own, other)
    return jnp.sum(exchange(mine + lax.ppermute(theirs, "ops", SWAP)), axis=0)


def sec_sum(values):
    row = jnp.pad(jnp.stack(values), (0, 128 - len(values)))[None]
    sums = jnp.sum(lax.all_to_all(jnp.broadcast_to(row[None], (16, 1, 128)), "sec", 0, 0), axis=(0, 1))
    return [sums[i] for i in range(len(values))]


def on_device(wavefunction, left_operators, right_operators, preconditioner, charges, coupling):
    entries = wavefunction.size * lax.axis_size("ops") * lax.axis_size("sec")
    position = lax.axis_index("sec")
    core = (lax.axis_index("ops") % 2).astype(jnp.int32)[None]
    edges = jnp.stack([position > 0, position < 15]).astype(jnp.int32)
    operators = (left_operators, right_operators, charges, coupling)
    slab = wavefunction.reshape(64, BLK)
    weights = preconditioner.reshape(64, BLK)

    own, other = gather(slab)
    summed = image(own, other, core, edges, *operators)
    image_psi = summed[:64]
    correlation, psi_norm = sec_sum([summed[64, 0], summed[65, 0]])
    scaled = (image_psi - correlation / psi_norm * slab) / weights

    sums = jnp.stack([jnp.sum(slab * scaled), jnp.sum(scaled * scaled)])
    sums = jnp.broadcast_to(jnp.pad(sums, (0, 6))[:, None], (8, BLK))
    own, other = gather(jnp.concatenate([scaled, sums]))
    totals = jnp.sum(own[:, 64:66, 0] + other[:, 64:66, 0], axis=0)
    projection, scaled_squares = sec_sum([totals[0], totals[1]])
    image_scaled = image(own, other, core, edges, *operators)[:64]

    along = projection / psi_norm
    squares = jnp.maximum(scaled_squares - along * projection, 0.0)
    size = jnp.sqrt(squares / entries + EPSILON)
    correction = (scaled - along * slab) / size
    image_new = (image_scaled - along * image_psi) / size
    return correction.reshape(wavefunction.shape), image_new.reshape(wavefunction.shape)


def solution(mesh):
    placed = (
        P("sec", "ops", None),
        P("ops", "sec", None, None),
        P("ops", "sec", None, None),
        P("sec", "ops", None),
        P("ops"),
        P("ops", "sec"),
    )
    return jax.shard_map(
        on_device,
        mesh=mesh,
        in_specs=placed,
        out_specs=(P("sec", "ops", None), P("sec", "ops", None)),
        check_vma=False,
    )
```

time: 630 us -> 176 us (0.28)
  waiting for transfers between devices: 253 us -> 29.9 us
  blocking collectives: 226 us -> 78.8 us
  matrix products: 50.1 us -> 0 us
  loops' own time: 33.8 us -> 0 us
  starting transfers between devices: 5.35 us -> 31.4 us
  local copies, waits for them, and re-layouts: 33.8 us -> 13.5 us
  between operations: 17.3 us -> 4.82 us
  Pallas kernels: 0 us -> 11.4 us
    psum x3 -> x0, blocking collectives: 226 us -> none  [the longest x1 79.7 us: on_device(): lax.psum((jnp.sum(wavefunction * wavefunction), jnp.sum(wavefunction * im...]
    reduce_scatter x2 -> x0, waiting for transfers between devices: 157 us -> none  [apply_operator(): lax.psum_scatter(fold_ghosts(extended), 'ops', scatter_dimension=1, tiled...]
    all_gather x2 -> x0, waiting for transfers between devices: 80.5 us -> none  [apply_operator(): blocks = lax.all_gather(slab, 'ops', axis=1, tiled=True)]
    all_to_all x0 -> x4, blocking collectives: none -> 78.8 us  [the longest x3 64.8 us: exchange(): return lax.all_to_all(parts, 'ops', 0, 0, axis_index_groups=SAME_CORE)]
    dot_general x36 -> x0, matrix products: 50.1 us -> none  [the longest x18 25.4 us: block_product(): jnp.dot(left_block, vector_block, precision=PRECISE, preferred_element_ty...]
    another operation x34 -> x0, loops' own time: 33.8 us -> none  [the longest x2 21.6 us: local_images(): return lax.fori_loop(0, term_count * pair_count, visit_item, starting)]
    dynamic_slice x50 -> x0, local copies, waits for them, and re-layouts: 31.4 us -> none  [the longest x32 20.1 us: visit_item(): coupling[term_index, pair_index] > 0]
    all_to_all x0 -> x2, waiting for transfers between devices: none -> 19.5 us  [the longest x1 14 us: exchange(): return lax.all_to_all(parts, 'ops', 0, 0, axis_index_groups=SAME_CORE)]
  transfers between devices with their start and end apart: 8 -> 10, of which waited for: 8 -> 7; matrix products, arithmetic and copies ran while one was open for 0% -> 2% of each run, Pallas kernels for 0% -> 3%
where the time goes in v1:
time: 176 us
  blocking collectives  78.8 us (45%)
  starting transfers between devices  31.4 us (18%)
  waiting for transfers between devices  29.9 us (17%)
  local copies, waits for them, and re-layouts  13.5 us (8%)
  Pallas kernels  11.4 us (6%)
  other arithmetic  6.01 us (3%)
  between operations  4.82 us (3%)
    all_to_all x3, blocking collectives, exchange(): return lax.all_to_all(parts, 'ops', 0, 0, axis_index_groups=SAME_CORE)  64.8 us
    all_to_all x1, waiting for transfers between devices, exchange(): return lax.all_to_all(parts, 'ops', 0, 0, axis_index_groups=SAME_CORE)  14 us
    all_to_all x1, blocking collectives, sec_sum(): lax.all_to_all(jnp.broadcast_to(row[None], (16, 1, 128)), 'sec', 0, 0)  14 us
    unnamed x20, local copies, waits for them, and re-layouts  10.1 us
    pallas_call x4, Pallas kernels, items(): pl.pallas_call(functools.partial(items_kernel, first, stride, start is no...  9.59 us
    all_to_all x1, starting transfers between devices, sec_sum(): lax.all_to_all(jnp.broadcast_to(row[None], (16, 1, 128)), 'sec', 0, 0)  7.32 us
    ppermute x2, starting transfers between devices, gather(): return (own, lax.ppermute(own, 'ops', SWAP))  6.45 us
    ppermute x2, starting transfers between devices, image(): from_low = lax.ppermute(high, 'sec', UP)  6.41 us
  transfers between devices with their start and end apart: 10, of which 7 were waited for; matrix products, arithmetic and copies ran while one was open for 2% of the time, Pallas kernels for 3%

profile of v1, /device:TPU:1, one launch (start us, length us, event | category | flops | bytes accessed | tf_op | source)
XLA Modules:
  0.0 175.8 jit_solution(944196940616628148)
XLA Ops:
  0.6 0.9 broadcast_in_dim.16
  1.5 24.8 %all_to_all.30.own = f32[8,64,256]{2,1,0:T(8,128)S(1)} all-to-all(f32[8,64,256]{2,1,0:T(8,128)S(1)} %broadcast_in_dim.16), channel_id=1, replica_groups={{0,32,64,96,128,160,192,224},{16,48,80,112,144,176,208,240},{1,33,65,97..., dimensions={0} | all-to-all | bytes 1048576 | tf_op jit(solution)/shard_map/all_to_all | solution.py:146
  26.3 2.5 %collective-permute-start = (f32[8,64,256]{2,1,0:T(8,128)S(1)}, f32[8,64,256]{2,1,0:T(8,128)S(1)}, u32[]{:S(2)}, u32[]{:S(2)}) collective-permute-start(f32[8,64,256]{2,1,0:T(8,128)S(1)} %all_to_all.30.own), channel_id=1, source_target_pairs={{0,16},{16,0},{32,48},{48,32},{64,80},{80,64},{96,112},{112,96},{1... | collective-permute-start | bytes 1572872 | tf_op jit(solution)/shard_map/ppermute | solution.py:151
  28.8 1.5 collective-permute-done.other
  30.3 0.0 copy-start
  30.3 2.2 %copy-done = f32[4,4,256,256]{3,2,1,0:T(8,128)S(1)} copy-done((f32[4,4,256,256]{3,2,1,0:T(8,128)S(1)}, f32[4,4,256,256]{3,2,1,0:T(8,128)}, u32[]{:S(2)}) %copy-start) | copy-done | bytes 4194328
  32.5 0.0 copy-start.2
  32.5 2.2 %copy-done.2 = f32[4,4,256,256]{3,2,1,0:T(8,128)S(1)} copy-done((f32[4,4,256,256]{3,2,1,0:T(8,128)S(1)}, f32[4,4,256,256]{3,2,1,0:T(8,128)}, u32[]{:S(2)}) %copy-start.2) | copy-done | bytes 4194328
  34.7 0.0 copy-start.4
  34.7 0.7 copy-done.4
  35.4 0.0 copy-start.6
  35.4 0.7 copy-done.6
  36.0 1.8 %shard_map.77 = (f32[4,256,256]{2,1,0:T(8,128)S(1)}, f32[256,256]{1,0:T(8,128)S(1)}, f32[256,256]{1,0:T(8,128)S(1)}) custom-call(s32[1]{0:T(128)} %bitcast.core, s32[4]{0:T(128)S(1)} %copy-done.6, s32[4,4]{1,0:T(4,128)S(1)} %copy-done.4, f32[4,4,256,256]{3,2,1,0:T(8,128)S(1)} %copy-done, f32[4,4,256,256]{3,2,1,0:T(8,128)S(1)} %copy-done.2, ...), custom_call_target="tpu_custom_call" | custom-call | flops 1610612736 | bytes 4194304 | tf_op jit(solution)/shard_map/pallas_call | solution.py:77
  37.9 3.7 %collective-permute-start.1 = (f32[256,256]{1,0:T(8,128)S(1)}, f32[256,256]{1,0:T(8,128)S(1)}, u32[]{:S(2)}, u32[]{:S(2)}) collective-permute-start(f32[256,256]{1,0:T(8,128)S(1)} %get-tuple-element.13), channel_id=1, source_target_pairs={{0,1},{1,2},{2,3},{3,4},{4,5},{5,6},{6,7},{7,8},{8,9},{9,10},{10,1... | collective-permute-start | bytes 786440 | tf_op jit(solution)/shard_map/ppermute | solution.py:157
  41.5 2.6 %collective-permute-start.2 = (f32[256,256]{1,0:T(8,128)S(1)}, f32[256,256]{1,0:T(8,128)S(1)}, u32[]{:S(2)}, u32[]{:S(2)}) collective-permute-start(f32[256,256]{1,0:T(8,128)S(1)} %get-tuple-element.14), channel_id=1, source_target_pairs={{0,15},{1,0},{2,1},{3,2},{4,3},{5,4},{6,5},{7,6},{8,7},{9,8},{10,9... | collective-permute-start | bytes 786440 | tf_op jit(solution)/shard_map/ppermute | solution.py:156
  44.2 0.1 add_convert_fusion.edges
  44.2 3.0 %shard_map.78.inner = f32[4,256,256]{2,1,0:T(8,128)S(1)} custom-call(s32[1]{0:T(128)} %bitcast.core, s32[4]{0:T(128)S(1)} %copy-done.6, s32[4,4]{1,0:T(4,128)S(1)} %copy-done.4, f32[4,4,256,256]{3,2,1,0:T(8,128)S(1)} %copy-done, f32[4,4,256,256]{3,2,1,0:T(8,128)S(1)} %copy-done.2, f32[8,64,256]{2,1,0:T(8,128)S(1)} %all_to_all.30.own, ...), custom_call_target="tpu_custom_call" | custom-call | flops 1610612736 | bytes 4194304 | tf_op jit(solution)/shard_map/pallas_call | solution.py:77
  47.2 0.0 copy-start.8
  47.2 0.0 copy-start.9
  47.2 0.0 copy-start.5
  47.2 0.0 copy-start.7
  47.3 3.2 %collective-permute-done.1.low = f32[256,256]{1,0:T(8,128)S(1)} collective-permute-done((f32[256,256]{1,0:T(8,128)S(1)}, f32[256,256]{1,0:T(8,128)S(1)}, u32[]{:S(2)}, u32[]{:S(2)}) %collective-permute-start.1) | collective-permute-done | bytes 262176 | tf_op jit(solution)/shard_map/ppermute | solution.py:157
  50.4 0.0 collective-permute-done.2.high
  50.4 0.9 shard_map.79
  51.3 1.0 collective-permute-start.3
  52.3 1.6 collective-permute-done.3
  53.9 0.1 add.24
  54.0 21.8 %all_to_all.31 = f32[8,72,256]{2,1,0:T(8,128)S(1)} all-to-all(f32[8,72,256]{2,1,0:T(8,128)S(1)} %add.24), channel_id=1, replica_groups={{0,32,64,96,128,160,192,224},{16,48,80,112,144,176,208,240},{1,33,65,97..., dimensions={0} | all-to-all | bytes 1179648 | tf_op jit(solution)/shard_map/all_to_all | solution.py:146
  75.8 0.6 fusion.4
  76.4 1.3 fusion.2
  77.7 14.0 %all_to_all.32 = f32[16,1,128]{2,1,0:T(1,128)S(1)} all-to-all(f32[16,1,128]{2,1,0:T(1,128)S(1)} %broadcast_in_dim.17), channel_id=1, replica_groups=mesh['ops'=16,'sec'=16] {'sec'}, dimensions={0} | all-to-all | bytes 16384 | tf_op jit(solution)/shard_map/all_to_all | solution.py:165
  91.8 0.6 fusion.6
  93.7 0.0 copy-done.8
  93.7 0.0 copy-done.9
  93.7 0.7 multiply_reduce_fusion.1
  94.4 1.3 fusion.3
  95.7 0.1 pad.15.clone
  95.8 0.1 pad_maximum_fusion
  95.9 18.2 %all_to_all.33.own = f32[8,72,256]{2,1,0:T(8,128)S(1)} all-to-all(f32[8,72,256]{2,1,0:T(8,128)S(1)} %broadcast_in_dim.37), channel_id=1, replica_groups={{0,32,64,96,128,160,192,224},{16,48,80,112,144,176,208,240},{1,33,65,97..., dimensions={0} | all-to-all | bytes 1179648 | tf_op jit(solution)/shard_map/all_to_all | solution.py:146
  114.2 4.0 %collective-permute-start.4 = (f32[8,72,256]{2,1,0:T(8,128)S(1)}, f32[8,72,256]{2,1,0:T(8,128)S(1)}, u32[]{:S(2)}, u32[]{:S(2)}) collective-permute-start(f32[8,72,256]{2,1,0:T(8,128)S(1)} %all_to_all.33.own), channel_id=1, source_target_pairs={{0,16},{16,0},{32,48},{48,32},{64,80},{80,64},{96,112},{112,96},{1... | collective-permute-start | bytes 1769480 | tf_op jit(solution)/shard_map/ppermute | solution.py:151
  118.2 1.6 collective-permute-done.4.other
  119.8 0.0 copy-done.5
  119.8 0.0 copy-done.7
  119.8 2.2 %copy-done.1 = f32[4,4,256,256]{3,2,1,0:T(8,128)S(1)} copy-done((f32[4,4,256,256]{3,2,1,0:T(8,128)S(1)}, f32[4,4,256,256]{3,2,1,0:T(8,128)}, u32[]{:S(2)}) %copy-start.1) | copy-done | bytes 4194328
  122.0 2.2 %copy-done.3 = f32[4,4,256,256]{3,2,1,0:T(8,128)S(1)} copy-done((f32[4,4,256,256]{3,2,1,0:T(8,128)S(1)}, f32[4,4,256,256]{3,2,1,0:T(8,128)}, u32[]{:S(2)}) %copy-start.3) | copy-done | bytes 4194328
  124.2 1.8 %shard_map.80 = (f32[4,256,256]{2,1,0:T(8,128)S(1)}, f32[256,256]{1,0:T(8,128)S(1)}, f32[256,256]{1,0:T(8,128)S(1)}) custom-call(s32[1]{0:T(128)} %bitcast.core, s32[4]{0:T(128)S(1)} %copy-done.7, s32[4,4]{1,0:T(4,128)S(1)} %copy-done.5, f32[4,4,256,256]{3,2,1,0:T(8,128)S(1)} %copy-done.1, f32[4,4,256,256]{3,2,1,0:T(8,128)S(1)} %copy-done.3, ...), custom_call_target="tpu_custom_call" | custom-call | flops 1610612736 | bytes 4194304 | tf_op jit(solution)/shard_map/pallas_call | solution.py:77
  126.0 2.7 %collective-permute-start.5 = (f32[256,256]{1,0:T(8,128)S(1)}, f32[256,256]{1,0:T(8,128)S(1)}, u32[]{:S(2)}, u32[]{:S(2)}) collective-permute-start(f32[256,256]{1,0:T(8,128)S(1)} %get-tuple-element.18), channel_id=1, source_target_pairs={{0,1},{1,2},{2,3},{3,4},{4,5},{5,6},{6,7},{7,8},{8,9},{9,10},{10,1... | collective-permute-start | bytes 786440 | tf_op jit(solution)/shard_map/ppermute | solution.py:157
  128.8 2.1 %collective-permute-start.6 = (f32[256,256]{1,0:T(8,128)S(1)}, f32[256,256]{1,0:T(8,128)S(1)}, u32[]{:S(2)}, u32[]{:S(2)}) collective-permute-start(f32[256,256]{1,0:T(8,128)S(1)} %get-tuple-element.19), channel_id=1, source_target_pairs={{0,15},{1,0},{2,1},{3,2},{4,3},{5,4},{6,5},{7,6},{8,7},{9,8},{10,9... | collective-permute-start | bytes 786440 | tf_op jit(solution)/shard_map/ppermute | solution.py:156
  130.9 3.0 %shard_map.81.inner = f32[4,256,256]{2,1,0:T(8,128)S(1)} custom-call(s32[1]{0:T(128)} %bitcast.core, s32[4]{0:T(128)S(1)} %copy-done.7, s32[4,4]{1,0:T(4,128)S(1)} %copy-done.5, f32[4,4,256,256]{3,2,1,0:T(8,128)S(1)} %copy-done.1, f32[4,4,256,256]{3,2,1,0:T(8,128)S(1)} %copy-done.3, f32[8,72,256]{2,1,0:T(8,128)S(1)} %all_to_all.33.own, ...), custom_call_target="tpu_custom_call" | custom-call | flops 1610612736 | bytes 4194304 | tf_op jit(solution)/shard_map/pallas_call | solution.py:77
  133.9 2.4 %collective-permute-done.5.low = f32[256,256]{1,0:T(8,128)S(1)} collective-permute-done((f32[256,256]{1,0:T(8,128)S(1)}, f32[256,256]{1,0:T(8,128)S(1)}, u32[]{:S(2)}, u32[]{:S(2)}) %collective-permute-start.5) | collective-permute-done | bytes 262176 | tf_op jit(solution)/shard_map/ppermute | solution.py:157
  136.3 0.0 collective-permute-done.6.high
  136.3 0.9 shard_map.82
  137.2 2.0 %collective-permute-start.7 = (f32[8,72,256]{2,1,0:T(8,128)S(1)}, f32[8,72,256]{2,1,0:T(8,128)S(1)}, u32[]{:S(2)}, u32[]{:S(2)}) collective-permute-start(f32[8,72,256]{2,1,0:T(8,128)S(1)} %get-tuple-element.21), channel_id=1, source_target_pairs={{0,16},{16,0},{32,48},{48,32},{64,80},{80,64},{96,112},{112,96},{1... | collective-permute-start | bytes 1769480 | tf_op jit(solution)/shard_map/ppermute | solution.py:160
  139.1 0.1 fusion.1
  139.3 0.6 broadcast_in_dim.38
  139.9 7.3 %all-to-all-start.4 = ((f32[16,1,128]{2,1,0:T(1,128)}), f32[16,1,128]{2,1,0:T(1,128)S(1)}, u32[]{:S(2)}, u32[]{:S(2)}) async-start(f32[16,1,128]{2,1,0:T(1,128)} %broadcast_in_dim.38), calls=%async_computation.4 | async-start | bytes 16384 | tf_op jit(solution)/shard_map/all_to_all | solution.py:165
  147.2 0.0 collective-permute-done.7
  147.2 0.9 add.27
  148.1 5.4 %all-to-all-done.4 = f32[16,1,128]{2,1,0:T(1,128)S(1)} async-done(((f32[16,1,128]{2,1,0:T(1,128)}), f32[16,1,128]{2,1,0:T(1,128)S(1)}, u32[]{:S(2)}, u32[]{:S(2)}) %all-to-all-start.4) | async-done | bytes 8224 | tf_op jit(solution)/shard_map/all_to_all | solution.py:165
  153.5 3.5 %all-to-all-start.5 = ((f32[8,72,256]{2,1,0:T(8,128)}), f32[8,72,256]{2,1,0:T(8,128)S(1)}, u32[]{:S(2)}, u32[]{:S(2)}) async-start(f32[8,72,256]{2,1,0:T(8,128)} %add.27), calls=%async_computation.5 | async-start | bytes 1179648 | tf_op jit(solution)/shard_map/all_to_all | solution.py:146
  157.1 0.6 fusion.5
  160.4 0.6 subtract_divide_fusion
  161.1 14.0 %all-to-all-done.5 = f32[8,72,256]{2,1,0:T(8,128)S(1)} async-done(((f32[8,72,256]{2,1,0:T(8,128)}), f32[8,72,256]{2,1,0:T(8,128)S(1)}, u32[]{:S(2)}, u32[]{:S(2)}) %all-to-all-start.5) | async-done | bytes 589856 | tf_op jit(solution)/shard_map/all_to_all | solution.py:146
  175.2 0.6 fusion
  (9 shorter events, 0.2 us)
Async XLA Ops:
  26.3 4.0 %collective-permute-start = (f32[8,64,256]{2,1,0:T(8,128)S(1)}, f32[8,64,256]{2,1,0:T(8,128)S(1)}, u32[]{:S(2)}, u32[]{:S(2)}) collective-permute-start(f32[8,64,256]{2,1,0:T(8,128)S(1)} %all_to_all.30.own), channel_id=1, source_target_pairs={{0,16},{16,0},{32,48},{48,32},{64,80},{80,64},{96,112},{112,96},{1... | collective-permute-start | bytes 1572872 | tf_op jit(solution)/shard_map/ppermute | solution.py:151
  30.3 2.2 %copy-start = (f32[4,4,256,256]{3,2,1,0:T(8,128)S(1)}, f32[4,4,256,256]{3,2,1,0:T(8,128)}, u32[]{:S(2)}) copy-start(f32[4,4,256,256]{3,2,1,0:T(8,128)} %left.7) | copy-start | bytes 12582916
  32.5 2.2 %copy-start.2 = (f32[4,4,256,256]{3,2,1,0:T(8,128)S(1)}, f32[4,4,256,256]{3,2,1,0:T(8,128)}, u32[]{:S(2)}) copy-start(f32[4,4,256,256]{3,2,1,0:T(8,128)} %right.7) | copy-start | bytes 12582916
  34.7 0.7 copy-start.4
  35.4 0.7 copy-start.6
  37.9 12.6 %collective-permute-start.1 = (f32[256,256]{1,0:T(8,128)S(1)}, f32[256,256]{1,0:T(8,128)S(1)}, u32[]{:S(2)}, u32[]{:S(2)}) collective-permute-start(f32[256,256]{1,0:T(8,128)S(1)} %get-tuple-element.13), channel_id=1, source_target_pairs={{0,1},{1,2},{2,3},{3,4},{4,5},{5,6},{6,7},{7,8},{8,9},{9,10},{10,1... | collective-permute-start | bytes 786440 | tf_op jit(solution)/shard_map/ppermute | solution.py:157
  41.5 8.9 %collective-permute-start.2 = (f32[256,256]{1,0:T(8,128)S(1)}, f32[256,256]{1,0:T(8,128)S(1)}, u32[]{:S(2)}, u32[]{:S(2)}) collective-permute-start(f32[256,256]{1,0:T(8,128)S(1)} %get-tuple-element.14), channel_id=1, source_target_pairs={{0,15},{1,0},{2,1},{3,2},{4,3},{5,4},{6,5},{7,6},{8,7},{9,8},{10,9... | collective-permute-start | bytes 786440 | tf_op jit(solution)/shard_map/ppermute | solution.py:156
  47.2 46.5 %copy-start.8 = (f32[4,16,256]{2,1,0:T(8,128)S(1)}, f32[4,16,256]{2,1,0:T(8,128)}, u32[]{:S(2)}) copy-start(f32[4,16,256]{2,1,0:T(8,128)} %param.6) | copy-start | bytes 196612
  47.2 46.5 %copy-start.9 = (f32[4,16,256]{2,1,0:T(8,128)S(1)}, f32[4,16,256]{2,1,0:T(8,128)}, u32[]{:S(2)}) copy-start(f32[4,16,256]{2,1,0:T(8,128)} %param.9) | copy-start | bytes 196612
  47.2 72.6 %copy-start.5 = (s32[4,4]{1,0:T(4,128)S(1)}, s32[4,4]{1,0:T(4,128)}, u32[]{:S(2)}) copy-start(s32[4,4]{1,0:T(4,128)} %coupling.7) | copy-start | bytes 196
  47.2 72.6 %copy-start.7 = (s32[4]{0:T(128)S(1)}, s32[4]{0:T(128)}, u32[]{:S(2)}) copy-start(s32[4]{0:T(128)} %charges.7) | copy-start | bytes 52
  51.3 2.6 %collective-permute-start.3 = (f32[8,72,256]{2,1,0:T(8,128)S(1)}, f32[8,72,256]{2,1,0:T(8,128)S(1)}, u32[]{:S(2)}, u32[]{:S(2)}) collective-permute-start(f32[8,72,256]{2,1,0:T(8,128)S(1)} %get-tuple-element.16), channel_id=1, source_target_pairs={{0,16},{16,0},{32,48},{48,32},{64,80},{80,64},{96,112},{112,96},{1... | collective-permute-start | bytes 1769480 | tf_op jit(solution)/shard_map/ppermute | solution.py:160
  114.2 5.6 %collective-permute-start.4 = (f32[8,72,256]{2,1,0:T(8,128)S(1)}, f32[8,72,256]{2,1,0:T(8,128)S(1)}, u32[]{:S(2)}, u32[]{:S(2)}) collective-permute-start(f32[8,72,256]{2,1,0:T(8,128)S(1)} %all_to_all.33.own), channel_id=1, source_target_pairs={{0,16},{16,0},{32,48},{48,32},{64,80},{80,64},{96,112},{112,96},{1... | collective-permute-start | bytes 1769480 | tf_op jit(solution)/shard_map/ppermute | solution.py:151
  119.8 2.2 %copy-start.1 = (f32[4,4,256,256]{3,2,1,0:T(8,128)S(1)}, f32[4,4,256,256]{3,2,1,0:T(8,128)}, u32[]{:S(2)}) copy-start(f32[4,4,256,256]{3,2,1,0:T(8,128)} %left.7) | copy-start | bytes 12582916
  122.0 2.2 %copy-start.3 = (f32[4,4,256,256]{3,2,1,0:T(8,128)S(1)}, f32[4,4,256,256]{3,2,1,0:T(8,128)}, u32[]{:S(2)}) copy-start(f32[4,4,256,256]{3,2,1,0:T(8,128)} %right.7) | copy-start | bytes 12582916
  126.0 10.2 %collective-permute-start.5 = (f32[256,256]{1,0:T(8,128)S(1)}, f32[256,256]{1,0:T(8,128)S(1)}, u32[]{:S(2)}, u32[]{:S(2)}) collective-permute-start(f32[256,256]{1,0:T(8,128)S(1)} %get-tuple-element.18), channel_id=1, source_target_pairs={{0,1},{1,2},{2,3},{3,4},{4,5},{5,6},{6,7},{7,8},{8,9},{9,10},{10,1... | collective-permute-start | bytes 786440 | tf_op jit(solution)/shard_map/ppermute | solution.py:157
  128.8 7.5 %collective-permute-start.6 = (f32[256,256]{1,0:T(8,128)S(1)}, f32[256,256]{1,0:T(8,128)S(1)}, u32[]{:S(2)}, u32[]{:S(2)}) collective-permute-start(f32[256,256]{1,0:T(8,128)S(1)} %get-tuple-element.19), channel_id=1, source_target_pairs={{0,15},{1,0},{2,1},{3,2},{4,3},{5,4},{6,5},{7,6},{8,7},{9,8},{10,9... | collective-permute-start | bytes 786440 | tf_op jit(solution)/shard_map/ppermute | solution.py:156
  137.2 10.0 %collective-permute-start.7 = (f32[8,72,256]{2,1,0:T(8,128)S(1)}, f32[8,72,256]{2,1,0:T(8,128)S(1)}, u32[]{:S(2)}, u32[]{:S(2)}) collective-permute-start(f32[8,72,256]{2,1,0:T(8,128)S(1)} %get-tuple-element.21), channel_id=1, source_target_pairs={{0,16},{16,0},{32,48},{48,32},{64,80},{80,64},{96,112},{112,96},{1... | collective-permute-start | bytes 1769480 | tf_op jit(solution)/shard_map/ppermute | solution.py:160
  139.9 13.7 %all-to-all-start.4 = ((f32[16,1,128]{2,1,0:T(1,128)}), f32[16,1,128]{2,1,0:T(1,128)S(1)}, u32[]{:S(2)}, u32[]{:S(2)}) async-start(f32[16,1,128]{2,1,0:T(1,128)} %broadcast_in_dim.38), calls=%async_computation.4 | async-start | bytes 16384 | tf_op jit(solution)/shard_map/all_to_all | solution.py:165
  153.5 21.6 %all-to-all-start.5 = ((f32[8,72,256]{2,1,0:T(8,128)}), f32[8,72,256]{2,1,0:T(8,128)S(1)}, u32[]{:S(2)}, u32[]{:S(2)}) async-start(f32[8,72,256]{2,1,0:T(8,128)} %add.27), calls=%async_computation.5 | async-start | bytes 1179648 | tf_op jit(solution)/shard_map/all_to_all | solution.py:146

commit v2 on v0

v2 whole, which is shorter than its diff:
```python
import functools

import jax
import jax.numpy as jnp
from jax import lax
from jax.experimental import pallas as pl
from jax.experimental.pallas import tpu as pltpu
from jax.sharding import PartitionSpec as P

EPSILON = 1e-06
F32 = jnp.float32
BF16 = jnp.bfloat16
BLK = 256
ROWS = 16
CORE, POSITION, CHARGES, COUPLING = 0, 1, 2, 6
NZ = 8
NT = (((1,), (1,)), ((), ()))
NN = (((1,), (0,)), ((), ()))
SMEM = pl.BlockSpec(memory_space=pltpu.SMEM)
VMEM = pl.BlockSpec(memory_space=pltpu.VMEM)
PARAMS = pltpu.CompilerParams(vmem_limit_bytes=24 * 1024 * 1024)


def shape(*dims, dtype=F32):
    return jax.ShapeDtypeStruct(dims, dtype)


def split(x):
    high = x.astype(BF16)
    return high, (x - high.astype(F32)).astype(BF16)


def dot(a, b, dims):
    return lax.dot_general(a, b, dims, preferred_element_type=F32)


def items(pairs, scalars, parts, own, other, acc):
    for slot, pair in enumerate(pairs):
        rows = slice(pair * ROWS, (pair + 1) * ROWS)
        pieces = []
        for z in range(NZ):
            a, b = own[z, rows, :], other[z, rows, :]
            pieces += [jnp.where(scalars[CORE] == 0, a, b), jnp.where(scalars[CORE] == 0, b, a)]
        vh, vl = split(jnp.concatenate(pieces, axis=0))
        for term in range(4):
            lh, ll, rh, rl = parts(slot, pair, term)
            uh, ul = split(dot(lh, vh, NN) + dot(lh, vl, NN) + dot(ll, vh, NN))
            acc[pair + 1 + scalars[CHARGES + term]] += dot(uh, rh, NT) + dot(uh, rl, NT) + dot(ul, rh, NT)


def kept_parts(left, right):
    return lambda slot, pair, term: (left[0, term, slot], left[1, term, slot], right[0, term, slot], right[1, term, slot])


EDGES, INNER = (0, 3), (1, 2)


def copies_of(pairs, left, right, blocks, semaphores):
    return [
        pltpu.make_async_copy(operator.at[term, pair], blocks.at[side, term, slot], semaphores.at[side, term, slot])
        for slot, pair in enumerate(pairs)
        for term in range(4)
        for side, operator in enumerate((left, right))
    ]


def fresh_parts(scalars, blocks, left_parts, right_parts):
    def parts(slot, pair, term):
        active = (scalars[COUPLING + 4 * term + pair] > 0).astype(F32)
        lh, ll = split(blocks[0, term, slot] * active)
        rh, rl = split(blocks[1, term, slot])
        left_parts[0, term, slot], left_parts[1, term, slot] = lh, ll
        right_parts[0, term, slot], right_parts[1, term, slot] = rh, rl
        return lh, ll, rh, rl

    return parts


def edge_parts_kernel(scalars, left, right, left_parts, right_parts, blocks, semaphores):
    copies = copies_of(EDGES, left, right, blocks, semaphores)
    for copy in copies:
        copy.start()
    parts = fresh_parts(scalars, blocks, left_parts, right_parts)
    for i, (slot, term) in enumerate((slot, term) for slot in range(2) for term in range(4)):
        copies[2 * i].wait()
        copies[2 * i + 1].wait()
        parts(slot, EDGES[slot], term)


def edges_of(acc, scalars, kept, given):
    kept[...] = acc[5 * scalars[CORE]]
    given[...] = acc[5 - 5 * scalars[CORE]]


def first_edge_kernel(scalars, left, right, left_parts, right_parts, own, other, acc, kept, given, blocks, semaphores):
    copies = copies_of(INNER, left, right, blocks, semaphores)
    for copy in copies:
        copy.start()
    acc[...] = jnp.zeros_like(acc)
    items(EDGES, scalars, kept_parts(left_parts, right_parts), own, other, acc)
    edges_of(acc, scalars, kept, given)
    for copy in copies:
        copy.wait()


def first_inner_kernel(scalars, blocks, own, other, start, acc, left_parts, right_parts):
    del start
    items(INNER, scalars, fresh_parts(scalars, blocks, left_parts, right_parts), own, other, acc)


def edge_kernel(scalars, left_parts, right_parts, own, other, acc, kept, given, totals):
    acc[...] = jnp.zeros_like(acc)
    items(EDGES, scalars, kept_parts(left_parts, right_parts), own, other, acc)
    edges_of(acc, scalars, kept, given)
    total = own[0, 64:72, :] + other[0, 64:72, :]
    for z in range(1, NZ):
        total += own[z, 64:72, :] + other[z, 64:72, :]
    totals[...] = total


def inner_kernel(scalars, left_parts, right_parts, own, other, start, acc):
    del start
    items(INNER, scalars, kept_parts(left_parts, right_parts), own, other, acc)


ACC, BLOCK = shape(6, BLK, BLK), shape(BLK, BLK)
BLOCKS = (2, 4, 2, BLK, BLK)
STAGED, PARTS = shape(*BLOCKS), shape(*BLOCKS, dtype=BF16)
COPIES = pltpu.SemaphoreType.DMA((2, 4, 2))


def on_blocks(kernel, outs, scalars, hbm, vmem, scratch=(), alias=None, flops=8 * 6 * 2 * BLK**3):
    return pl.pallas_call(
        kernel,
        in_specs=[SMEM] + [pl.BlockSpec(memory_space=pltpu.HBM)] * len(hbm) + [VMEM] * len(vmem),
        out_specs=[VMEM] * len(outs),
        out_shape=outs,
        scratch_shapes=scratch,
        input_output_aliases=alias or {},
        compiler_params=PARAMS,
        cost_estimate=pl.CostEstimate(flops=flops, bytes_accessed=8 * 2**19, transcendentals=0),
    )(scalars, *hbm, *vmem)


def arrange_kernel(scalars, acc, edge, own, other, *rest):
    *carried, mine, theirs = rest
    from_low = (scalars[CORE] == 1) & (scalars[POSITION] > 0)
    from_high = (scalars[CORE] == 0) & (scalars[POSITION] < 15)
    dots = jnp.zeros((8, BLK), F32)
    norms = jnp.zeros((8, BLK), F32)
    for pair in range(4):
        for z in range(NZ):
            pieces = []
            for half in range(2):
                rows = slice((2 * z + half) * ROWS, (2 * z + half + 1) * ROWS)
                piece = acc[pair + 1, rows, :]
                if pair == 0:
                    piece = piece + jnp.where(from_low, edge[rows, :], 0.0)
                if pair == 3:
                    piece = piece + jnp.where(from_high, edge[rows, :], 0.0)
                pieces.append(piece)
            place = slice(pair * ROWS, (pair + 1) * ROWS)
            a = jnp.where(scalars[CORE] == 0, pieces[0], pieces[1])
            b = jnp.where(scalars[CORE] == 0, pieces[1], pieces[0])
            mine[z, place, :] = a
            theirs[z, place, :] = b
            if not carried:
                va, vb = own[z, place, :], other[z, place, :]
                d = a * va + b * vb
                n = va * va + vb * vb
                dots += d[:8] + d[8:]
                norms += n[:8] + n[8:]
    if carried:
        sums = carried[0][...]
    else:
        row = lax.broadcasted_iota(jnp.int32, (8, BLK), 0)
        sums = jnp.where(row == 0, jnp.sum(dots), 0.0) + jnp.where(row == 1, jnp.sum(norms) * (1.0 / 16), 0.0)
    for z in range(NZ):
        mine[z, 64:72, :] = sums
        theirs[z, 64:72, :] = sums


def arrange(scalars, acc, edge, own, other, *carried):
    return pl.pallas_call(
        arrange_kernel,
        in_specs=[SMEM] + [VMEM] * (4 + len(carried)),
        out_specs=[VMEM, VMEM],
        out_shape=[shape(NZ, 72, BLK)] * 2,
        compiler_params=PARAMS,
    )(scalars, acc, edge, own, other, *carried)


def added(parts):
    total = parts[0]
    for z in range(1, NZ):
        total += parts[z]
    return total


def image_kernel(parts, image, sums):
    total = added(parts)
    image[...] = total[:64]
    for i in range(16):
        sums[i] = total[64:72, :128]


def scaled_kernel(parts, image, vector, weights, scaled, norm, sent):
    sums = parts[0]
    for i in range(1, 16):
        sums += parts[i]
    rayleigh = sums[0:1, 0:1] / sums[1:2, 0:1]
    norm[...] = jnp.broadcast_to(sums[1:2, 0:1], (8, BLK))
    value = (image[...] - rayleigh * vector[...]) / weights[...]
    scaled[...] = value
    row = lax.broadcasted_iota(jnp.int32, (8, BLK), 0)
    along = jnp.where(row == 0, jnp.sum(vector[...] * value), 0.0)
    rows = along + jnp.where(row == 1, jnp.sum(value * value), 0.0)
    for z in range(NZ):
        sent[z, :64, :] = value
        sent[z, 64:72, :] = rows


def finish_kernel(entries, parts, image, vector, scaled, norm, correction, image_new):
    total = added(parts)
    projection, squares = total[64:65, 0:1], total[65:66, 0:1]
    along = projection / norm[0:1, 0:1]
    squares = jnp.maximum(squares - along * projection, 0.0)
    size = jnp.sqrt(squares / entries + EPSILON)
    correction[...] = (scaled[...] - along * vector[...]) / size
    image_new[...] = (total[:64] - along * image[...]) / size


def local(kernel, outs, *args):
    return pl.pallas_call(
        kernel, in_specs=[VMEM] * len(args), out_specs=[VMEM] * len(outs), out_shape=outs, compiler_params=PARAMS
    )(*args)


SWAP = [(i, i ^ 1) for i in range(16)]
SAME_CORE = [[2 * z + c for z in range(NZ)] for c in range(2)]
TO_EDGES = [(o * 16 + s, o * 16 + (s + 2 * (o % 2) - 1) % 16) for o in range(16) for s in range(16)]
DIAGONAL = [(o * 16 + (s + o) % 16, o * 16 + s) for o in range(16) for s in range(16)]


def exchange(parts):
    return lax.all_to_all(parts, "ops", 0, 0, axis_index_groups=SAME_CORE)


def on_device(wavefunction, left_operators, right_operators, preconditioner, charges, coupling):
    entries = wavefunction.size * lax.axis_size("ops") * lax.axis_size("sec")
    core, position = lax.axis_index("ops") % 2, lax.axis_index("sec")
    scalars = jnp.concatenate([jnp.stack([core, position]).astype(jnp.int32), charges, coupling.reshape(16)])
    slab = wavefunction.reshape(64, BLK)
    weights = preconditioner.reshape(64, BLK)
    slab, scalars = lax.optimization_barrier((slab, scalars))
    operators = [pltpu.with_memory_space_constraint(x, pltpu.HBM) for x in (left_operators, right_operators)]

    def combined(acc, edge, own, other, *carried):
        mine, theirs = arrange(scalars, acc, edge, own, other, *carried)
        return exchange(mine + lax.ppermute(theirs, "ops", SWAP))

    def to_neighbour(kept, given):
        return lax.ppermute(kept + lax.ppermute(given, "ops", SWAP), ("ops", "sec"), TO_EDGES)

    own = exchange(jnp.broadcast_to(slab[None], (NZ, 64, BLK)))
    other = lax.ppermute(own, "ops", SWAP)
    scratch = [pltpu.VMEM(BLOCKS, F32), COPIES]
    edge_parts = on_blocks(edge_parts_kernel, [PARTS] * 2, scalars, operators, [], scratch, flops=0)
    outs = [ACC, BLOCK, BLOCK, STAGED]
    vectors = [*edge_parts, own, other]
    acc, kept, given, staged = on_blocks(first_edge_kernel, outs, scalars, operators, vectors, [COPIES])
    edge = to_neighbour(kept, given)
    outs, vectors = [ACC, PARTS, PARTS], [staged, own, other, acc]
    acc, *inner_parts = on_blocks(first_inner_kernel, outs, scalars, [], vectors, alias={4: 0})
    parts = combined(acc, edge, own, other)

    image, sums = local(image_kernel, [shape(64, BLK), shape(16, 8, 128)], parts)
    sums = lax.all_to_all(sums, "sec", 0, 0)
    outs = [shape(64, BLK), shape(8, BLK), shape(NZ, 72, BLK)]
    scaled, norm, sent = local(scaled_kernel, outs, sums, image, slab, weights)

    own = exchange(sent)
    other = lax.ppermute(own, "ops", SWAP)
    outs = [ACC, BLOCK, BLOCK, shape(8, BLK)]
    acc, kept, given, totals = on_blocks(edge_kernel, outs, scalars, [], [*edge_parts, own, other])
    edge = to_neighbour(kept, given)
    totals = lax.ppermute(totals, ("ops", "sec"), DIAGONAL)
    (acc,) = on_blocks(inner_kernel, [ACC], scalars, [], [*inner_parts, own, other, acc], alias={5: 0})
    parts = combined(acc, edge, own, other, totals)
    finish = functools.partial(finish_kernel, float(entries))
    correction, image_new = local(finish, [shape(64, BLK)] * 2, parts, image, slab, scaled, norm)
    return correction.reshape(wavefunction.shape), image_new.reshape(wavefunction.shape)


def solution(mesh):
    placed = (
        P("sec", "ops", None),
        P("ops", "sec", None, None),
        P("ops", "sec", None, None),
        P("sec", "ops", None),
        P("ops"),
        P("ops", "sec"),
    )
    return jax.shard_map(
        on_device,
        mesh=mesh,
        in_specs=placed,
        out_specs=(P("sec", "ops", None), P("sec", "ops", None)),
        check_vma=False,
    )
```

time: 630 us -> 150 us (0.24)
  waiting for transfers between devices: 253 us -> 12.7 us
  blocking collectives: 226 us -> 99.6 us
  matrix products: 50.1 us -> 0 us
  loops' own time: 33.8 us -> 0 us
  local copies, waits for them, and re-layouts: 33.8 us -> 1.65 us
  Pallas kernels: 0 us -> 18.3 us
  between operations: 17.3 us -> 0.79 us
  starting transfers between devices: 5.35 us -> 16 us
    psum x3 -> x0, blocking collectives: 226 us -> none  [the longest x1 79.7 us: on_device(): lax.psum((jnp.sum(wavefunction * wavefunction), jnp.sum(wavefunction * im...]
    reduce_scatter x2 -> x0, waiting for transfers between devices: 157 us -> none  [apply_operator(): lax.psum_scatter(fold_ghosts(extended), 'ops', scatter_dimension=1, tiled...]
    all_to_all x0 -> x5, blocking collectives: none -> 99.6 us  [the longest x4 86.4 us: exchange(): return lax.all_to_all(parts, 'ops', 0, 0, axis_index_groups=SAME_CORE)]
    all_gather x2 -> x0, waiting for transfers between devices: 80.5 us -> none  [apply_operator(): blocks = lax.all_gather(slab, 'ops', axis=1, tiled=True)]
    dot_general x36 -> x0, matrix products: 50.1 us -> none  [the longest x18 25.4 us: block_product(): jnp.dot(left_block, vector_block, precision=PRECISE, preferred_element_ty...]
    another operation x34 -> x0, loops' own time: 33.8 us -> none  [the longest x2 21.6 us: local_images(): return lax.fori_loop(0, term_count * pair_count, visit_item, starting)]
    dynamic_slice x50 -> x0, local copies, waits for them, and re-layouts: 31.4 us -> none  [the longest x32 20.1 us: visit_item(): coupling[term_index, pair_index] > 0]
    pallas_call x0 -> x10, Pallas kernels: none -> 18.3 us  [the longest x5 15.8 us: on_blocks(): pl.pallas_call(kernel, in_specs=[SMEM] + [pl.BlockSpec(memory_space=pltpu...]
  transfers between devices with their start and end apart: 8 -> 9, of which waited for: 8 -> 6; matrix products, arithmetic and copies ran while one was open for 0% -> 0% of each run, Pallas kernels for 0% -> 6%
where the time goes in v2:
time: 150 us
  blocking collectives  99.6 us (66%)
  Pallas kernels  18.3 us (12%)
  starting transfers between devices  16 us (11%)
  waiting for transfers between devices  12.7 us (8%)
  local copies, waits for them, and re-layouts  1.65 us (1%)
    all_to_all x4, blocking collectives, exchange(): return lax.all_to_all(parts, 'ops', 0, 0, axis_index_groups=SAME_CORE)  86.4 us
    pallas_call x5, Pallas kernels, on_blocks(): pl.pallas_call(kernel, in_specs=[SMEM] + [pl.BlockSpec(memory_space=pltpu...  15.8 us
    all_to_all x1, blocking collectives, on_device(): sums = lax.all_to_all(sums, 'sec', 0, 0)  13.2 us
    ppermute x2, starting transfers between devices, on_device(): other = lax.ppermute(own, 'ops', SWAP)  6.45 us
    ppermute x1, starting transfers between devices, on_device(): totals = lax.ppermute(totals, ('ops', 'sec'), DIAGONAL)  6.21 us
    ppermute x2, waiting for transfers between devices, to_neighbour(): lax.ppermute(kept + lax.ppermute(given, 'ops', SWAP), ('ops', 'sec'), TO_...  4.72 us
    ppermute x2, waiting for transfers between devices, combined(): return exchange(mine + lax.ppermute(theirs, 'ops', SWAP))  3.62 us
  transfers between devices with their start and end apart: 9, of which 6 were waited for; matrix products, arithmetic and copies ran while one was open for 0% of the time, Pallas kernels for 6%

profile of v2, /device:TPU:1, one launch (start us, length us, event | category | flops | bytes accessed | tf_op | source)
XLA Modules:
  0.0 149.9 jit_solution(17621451047068206840)
XLA Ops:
  0.6 0.8 reshape.21
  1.4 0.7 pad_add_fusion.scalars
  2.1 0.9 broadcast_in_dim.2
  3.0 24.8 %all_to_all.25.own = f32[8,64,256]{2,1,0:T(8,128)S(1)} all-to-all(f32[8,64,256]{2,1,0:T(8,128)S(1)} %broadcast_in_dim.2), channel_id=1, replica_groups={{0,32,64,96,128,160,192,224},{16,48,80,112,144,176,208,240},{1,33,65,97..., dimensions={0} | all-to-all | bytes 1048576 | tf_op jit(solution)/shard_map/all_to_all | solution.py:246
  27.8 2.5 %collective-permute-start = (f32[8,64,256]{2,1,0:T(8,128)S(1)}, f32[8,64,256]{2,1,0:T(8,128)S(1)}, u32[]{:S(2)}, u32[]{:S(2)}) collective-permute-start(f32[8,64,256]{2,1,0:T(8,128)S(1)} %all_to_all.25.own), channel_id=1, source_target_pairs={{0,16},{16,0},{32,48},{48,32},{64,80},{80,64},{96,112},{112,96},{1... | collective-permute-start | bytes 1572872 | tf_op jit(solution)/shard_map/ppermute | solution.py:266
  30.3 2.9 %shard_map.77 = (bf16[2,4,2,256,256]{4,3,2,1,0:T(8,128)(2,1)S(1)}, bf16[2,4,2,256,256]{4,3,2,1,0:T(8,128)(2,1)S(1)}) custom-call(s32[22]{0:T(128)S(1)} %pad_add_fusion.scalars, f32[4,4,256,256]{3,2,1,0:T(8,128)} %left.3, f32[4,4,256,256]{3,2,1,0:T(8,128)} %right.3), custom_call_target="tpu_custom_call" | custom-call | bytes 4194304 | tf_op jit(solution)/shard_map/pallas_call | solution.py:133
  33.2 0.0 collective-permute-done.other
  33.2 4.7 %shard_map.78 = (f32[6,256,256]{2,1,0:T(8,128)S(1)}, f32[256,256]{1,0:T(8,128)S(1)}, f32[256,256]{1,0:T(8,128)S(1)}, f32[2,4,2,256,256]{4,3,2,1,0:T(8,128)S(1)}) custom-call(s32[22]{0:T(128)S(1)} %pad_add_fusion.scalars, f32[4,4,256,256]{3,2,1,0:T(8,128)} %left.3, f32[4,4,256,256]{3,2,1,0:T(8,128)} %right.3, ...), custom_call_target="tpu_custom_call" | custom-call | flops 1610612736 | bytes 4194304 | tf_op jit(solution)/shard_map/pallas_call | solution.py:133
  37.9 0.1 collective-permute-start.1
  38.0 1.5 %collective-permute-done.1 = f32[256,256]{1,0:T(8,128)S(1)} collective-permute-done((f32[256,256]{1,0:T(8,128)S(1)}, f32[256,256]{1,0:T(8,128)S(1)}, u32[]{:S(2)}, u32[]{:S(2)}) %collective-permute-start.1) | collective-permute-done | bytes 262176 | tf_op jit(solution)/shard_map/ppermute | solution.py:263
  39.5 1.3 collective-permute-start.2
  40.8 2.8 %shard_map.79 = (f32[6,256,256]{2,1,0:T(8,128)S(1)}, bf16[2,4,2,256,256]{4,3,2,1,0:T(8,128)(2,1)S(1)}, bf16[2,4,2,256,256]{4,3,2,1,0:T(8,128)(2,1)S(1)}) custom-call(s32[22]{0:T(128)S(1)} %pad_add_fusion.scalars, f32[2,4,2,256,256]{4,3,2,1,0:T(8,128)S(1)} %get-tuple-element.32.blocks, ...), custom_call_target="tpu_custom_call", output_to_operand_aliasing={{0}: (4, {})} | custom-call | flops 1610612736 | bytes 4194304 | tf_op jit(solution)/shard_map/pallas_call | solution.py:133
  43.6 4.7 %collective-permute-done.2.edge = f32[256,256]{1,0:T(8,128)S(1)} collective-permute-done((f32[256,256]{1,0:T(8,128)S(1)}, f32[256,256]{1,0:T(8,128)S(1)}, u32[]{:S(2)}, u32[]{:S(2)}) %collective-permute-start.2) | collective-permute-done | bytes 262176 | tf_op jit(solution)/shard_map/ppermute | solution.py:263
  48.3 0.9 shard_map.80
  49.2 0.0 copy-start
  49.2 0.0 copy-start.1
  49.2 0.6 collective-permute-start.3
  49.9 1.6 %collective-permute-done.3 = f32[8,72,256]{2,1,0:T(8,128)S(1)} collective-permute-done((f32[8,72,256]{2,1,0:T(8,128)S(1)}, f32[8,72,256]{2,1,0:T(8,128)S(1)}, u32[]{:S(2)}, u32[]{:S(2)}) %collective-permute-start.3) | collective-permute-done | bytes 589856 | tf_op jit(solution)/shard_map/ppermute | solution.py:260
  51.5 0.1 add.18
  51.6 21.8 %all_to_all.26.parts = f32[8,72,256]{2,1,0:T(8,128)S(1)} all-to-all(f32[8,72,256]{2,1,0:T(8,128)S(1)} %add.18), channel_id=1, replica_groups={{0,32,64,96,128,160,192,224},{16,48,80,112,144,176,208,240},{1,33,65,97..., dimensions={0} | all-to-all | bytes 1179648 | tf_op jit(solution)/shard_map/all_to_all | solution.py:246
  73.4 13.2 %all_to_all.27.parts = f32[16,8,128]{2,1,0:T(8,128)S(1)} all-to-all(f32[16,8,128]{2,1,0:T(8,128)S(1)} %get-tuple-element.41), channel_id=1, replica_groups=mesh['ops'=16,'sec'=16] {'sec'}, dimensions={0} | all-to-all | bytes 131072 | tf_op jit(solution)/shard_map/all_to_all | solution.py:278
  86.6 0.0 copy-done
  86.6 0.0 copy-done.1
  86.6 0.2 shard_map.82
  86.8 18.2 %all_to_all.28.own = f32[8,72,256]{2,1,0:T(8,128)S(1)} all-to-all(f32[8,72,256]{2,1,0:T(8,128)S(1)} %get-tuple-element.43), channel_id=1, replica_groups={{0,32,64,96,128,160,192,224},{16,48,80,112,144,176,208,240},{1,33,65,97..., dimensions={0} | all-to-all | bytes 1179648 | tf_op jit(solution)/shard_map/all_to_all | solution.py:246
  105.0 4.0 %collective-permute-start.4 = (f32[8,72,256]{2,1,0:T(8,128)S(1)}, f32[8,72,256]{2,1,0:T(8,128)S(1)}, u32[]{:S(2)}, u32[]{:S(2)}) collective-permute-start(f32[8,72,256]{2,1,0:T(8,128)S(1)} %all_to_all.28.own), channel_id=1, source_target_pairs={{0,16},{16,0},{32,48},{48,32},{64,80},{80,64},{96,112},{112,96},{1... | collective-permute-start | bytes 1769480 | tf_op jit(solution)/shard_map/ppermute | solution.py:283
  109.0 1.6 %collective-permute-done.4.other = f32[8,72,256]{2,1,0:T(8,128)S(1)} collective-permute-done((f32[8,72,256]{2,1,0:T(8,128)S(1)}, f32[8,72,256]{2,1,0:T(8,128)S(1)}, u32[]{:S(2)}, u32[]{:S(2)}) %collective-permute-start.4) | collective-permute-done | bytes 589856 | tf_op jit(solution)/shard_map/ppermute | solution.py:283
  110.7 2.8 %shard_map.83 = (f32[6,256,256]{2,1,0:T(8,128)S(1)}, f32[256,256]{1,0:T(8,128)S(1)}, f32[256,256]{1,0:T(8,128)S(1)}, f32[8,256]{1,0:T(8,128)S(1)}) custom-call(s32[22]{0:T(128)S(1)} %pad_add_fusion.scalars, bf16[2,4,2,256,256]{4,3,2,1,0:T(8,128)(2,1)S(1)} %get-tuple-element.29.left_parts, bf16[2,4,2,256,256]{4,3,2,1,0:T(8,128)(2,1)S(1)} %get-tuple-element.30.right_parts, ...), custom_call_target="tpu_custom_call" | custom-call | flops 1610612736 | bytes 4194304 | tf_op jit(solution)/shard_map/pallas_call | solution.py:133
  113.5 0.5 collective-permute-start.5
  113.9 1.2 collective-permute-done.5
  115.1 0.7 collective-permute-start.6
  115.8 6.2 %collective-permute-start.7 = (f32[8,256]{1,0:T(8,128)S(1)}, f32[8,256]{1,0:T(8,128)S(1)}, u32[]{:S(2)}, u32[]{:S(2)}) collective-permute-start(f32[8,256]{1,0:T(8,128)S(1)} %get-tuple-element.47), channel_id=1, source_target_pairs={{0,0},{1,1},{2,2},{3,3},{4,4},{5,5},{6,6},{7,7},{8,8},{9,9},{10,10... | collective-permute-start | bytes 24584 | tf_op jit(solution)/shard_map/ppermute | solution.py:287
  122.1 2.7 %shard_map.84.acc = f32[6,256,256]{2,1,0:T(8,128)S(1)} custom-call(s32[22]{0:T(128)S(1)} %pad_add_fusion.scalars, bf16[2,4,2,256,256]{4,3,2,1,0:T(8,128)(2,1)S(1)} %get-tuple-element.34.left_parts, bf16[2,4,2,256,256]{4,3,2,1,0:T(8,128)(2,1)S(1)} %get-tuple-element.35.right_parts, f32[8,72,256]{2,1,0:T(8,128)S(1)} %all_to_all.28.own, ...), custom_call_target="tpu_custom_call", output_to_operand_aliasing={{}: (5, {})} | custom-call | flops 1610612736 | bytes 4194304 | tf_op jit(solution)/shard_map/pallas_call | solution.py:133
  124.7 0.0 collective-permute-done.7.rest_0_
  124.7 0.0 collective-permute-done.6.edge
  124.8 0.7 shard_map.85
  125.4 0.1 collective-permute-start.8
  125.5 2.0 %collective-permute-done.8 = f32[8,72,256]{2,1,0:T(8,128)S(1)} collective-permute-done((f32[8,72,256]{2,1,0:T(8,128)S(1)}, f32[8,72,256]{2,1,0:T(8,128)S(1)}, u32[]{:S(2)}, u32[]{:S(2)}) %collective-permute-start.8) | collective-permute-done | bytes 589856 | tf_op jit(solution)/shard_map/ppermute | solution.py:260
  127.5 0.1 add.20
  127.6 21.6 %all_to_all.29.parts = f32[8,72,256]{2,1,0:T(8,128)S(1)} all-to-all(f32[8,72,256]{2,1,0:T(8,128)S(1)} %add.20), channel_id=1, replica_groups={{0,32,64,96,128,160,192,224},{16,48,80,112,144,176,208,240},{1,33,65,97..., dimensions={0} | all-to-all | bytes 1179648 | tf_op jit(solution)/shard_map/all_to_all | solution.py:246
  149.2 0.7 shard_map.86
  (3 shorter events, 0.1 us)
Async XLA Ops:
  27.8 5.4 %collective-permute-start = (f32[8,64,256]{2,1,0:T(8,128)S(1)}, f32[8,64,256]{2,1,0:T(8,128)S(1)}, u32[]{:S(2)}, u32[]{:S(2)}) collective-permute-start(f32[8,64,256]{2,1,0:T(8,128)S(1)} %all_to_all.25.own), channel_id=1, source_target_pairs={{0,16},{16,0},{32,48},{48,32},{64,80},{80,64},{96,112},{112,96},{1... | collective-permute-start | bytes 1572872 | tf_op jit(solution)/shard_map/ppermute | solution.py:266
  37.9 1.6 %collective-permute-start.1 = (f32[256,256]{1,0:T(8,128)S(1)}, f32[256,256]{1,0:T(8,128)S(1)}, u32[]{:S(2)}, u32[]{:S(2)}) collective-permute-start(f32[256,256]{1,0:T(8,128)S(1)} %get-tuple-element.38), channel_id=1, source_target_pairs={{0,16},{16,0},{32,48},{48,32},{64,80},{80,64},{96,112},{112,96},{1... | collective-permute-start | bytes 786440 | tf_op jit(solution)/shard_map/ppermute | solution.py:263
  39.5 8.8 %collective-permute-start.2 = (f32[256,256]{1,0:T(8,128)S(1)}, f32[256,256]{1,0:T(8,128)S(1)}, u32[]{:S(2)}, u32[]{:S(2)}) collective-permute-start(f32[256,256]{1,0:T(8,128)S(1)} %add.17), channel_id=1, source_target_pairs={{0,15},{1,0},{2,1},{3,2},{4,3},{5,4},{6,5},{7,6},{8,7},{9,8},{10,9... | collective-permute-start | bytes 786440 | tf_op jit(solution)/shard_map/ppermute | solution.py:263
  49.2 37.4 %copy-start = (f32[4,16,256]{2,1,0:T(8,128)S(1)}, f32[4,16,256]{2,1,0:T(8,128)}, u32[]{:S(2)}) copy-start(f32[4,16,256]{2,1,0:T(8,128)} %param.6) | copy-start | bytes 196612
  49.2 37.4 %copy-start.1 = (f32[4,16,256]{2,1,0:T(8,128)S(1)}, f32[4,16,256]{2,1,0:T(8,128)}, u32[]{:S(2)}) copy-start(f32[4,16,256]{2,1,0:T(8,128)} %param.9) | copy-start | bytes 196612
  49.2 2.3 %collective-permute-start.3 = (f32[8,72,256]{2,1,0:T(8,128)S(1)}, f32[8,72,256]{2,1,0:T(8,128)S(1)}, u32[]{:S(2)}, u32[]{:S(2)}) collective-permute-start(f32[8,72,256]{2,1,0:T(8,128)S(1)} %get-tuple-element.40), channel_id=1, source_target_pairs={{0,16},{16,0},{32,48},{48,32},{64,80},{80,64},{96,112},{112,96},{1... | collective-permute-start | bytes 1769480 | tf_op jit(solution)/shard_map/ppermute | solution.py:260
  105.0 5.6 %collective-permute-start.4 = (f32[8,72,256]{2,1,0:T(8,128)S(1)}, f32[8,72,256]{2,1,0:T(8,128)S(1)}, u32[]{:S(2)}, u32[]{:S(2)}) collective-permute-start(f32[8,72,256]{2,1,0:T(8,128)S(1)} %all_to_all.28.own), channel_id=1, source_target_pairs={{0,16},{16,0},{32,48},{48,32},{64,80},{80,64},{96,112},{112,96},{1... | collective-permute-start | bytes 1769480 | tf_op jit(solution)/shard_map/ppermute | solution.py:283
  113.5 1.6 %collective-permute-start.5 = (f32[256,256]{1,0:T(8,128)S(1)}, f32[256,256]{1,0:T(8,128)S(1)}, u32[]{:S(2)}, u32[]{:S(2)}) collective-permute-start(f32[256,256]{1,0:T(8,128)S(1)} %get-tuple-element.46), channel_id=1, source_target_pairs={{0,16},{16,0},{32,48},{48,32},{64,80},{80,64},{96,112},{112,96},{1... | collective-permute-start | bytes 786440 | tf_op jit(solution)/shard_map/ppermute | solution.py:263
  115.1 9.6 %collective-permute-start.6 = (f32[256,256]{1,0:T(8,128)S(1)}, f32[256,256]{1,0:T(8,128)S(1)}, u32[]{:S(2)}, u32[]{:S(2)}) collective-permute-start(f32[256,256]{1,0:T(8,128)S(1)} %add.19), channel_id=1, source_target_pairs={{0,15},{1,0},{2,1},{3,2},{4,3},{5,4},{6,5},{7,6},{8,7},{9,8},{10,9... | collective-permute-start | bytes 786440 | tf_op jit(solution)/shard_map/ppermute | solution.py:263
  115.8 8.9 %collective-permute-start.7 = (f32[8,256]{1,0:T(8,128)S(1)}, f32[8,256]{1,0:T(8,128)S(1)}, u32[]{:S(2)}, u32[]{:S(2)}) collective-permute-start(f32[8,256]{1,0:T(8,128)S(1)} %get-tuple-element.47), channel_id=1, source_target_pairs={{0,0},{1,1},{2,2},{3,3},{4,4},{5,5},{6,6},{7,7},{8,8},{9,9},{10,10... | collective-permute-start | bytes 24584 | tf_op jit(solution)/shard_map/ppermute | solution.py:287
  125.4 2.1 %collective-permute-start.8 = (f32[8,72,256]{2,1,0:T(8,128)S(1)}, f32[8,72,256]{2,1,0:T(8,128)S(1)}, u32[]{:S(2)}, u32[]{:S(2)}) collective-permute-start(f32[8,72,256]{2,1,0:T(8,128)S(1)} %get-tuple-element.49), channel_id=1, source_target_pairs={{0,16},{16,0},{32,48},{48,32},{64,80},{80,64},{96,112},{112,96},{1... | collective-permute-start | bytes 1769480 | tf_op jit(solution)/shard_map/ppermute | solution.py:260

commit v3 on v2

v3 whole, which is shorter than its diff:
```python
import functools

import jax
import jax.numpy as jnp
from jax import lax
from jax.experimental import pallas as pl
from jax.experimental.pallas import tpu as pltpu
from jax.sharding import PartitionSpec as P

EPSILON = 1e-06
F32 = jnp.float32
BF16 = jnp.bfloat16
BLK = 256
ROWS = 16
NZ = 8
NT = (((1,), (1,)), ((), ()))
NN = (((1,), (0,)), ((), ()))
SMEM = pl.BlockSpec(memory_space=pltpu.SMEM)
VMEM = pl.BlockSpec(memory_space=pltpu.VMEM)
PARAMS = pltpu.CompilerParams(vmem_limit_bytes=24 * 1024 * 1024)


def shape(*dims, dtype=F32):
    return jax.ShapeDtypeStruct(dims, dtype)


def split(x):
    high = x.astype(BF16)
    return high, (x - high.astype(F32)).astype(BF16)


def dot(a, b, dims):
    return lax.dot_general(a, b, dims, preferred_element_type=F32)


def items(pairs, scalars, parts, own, other, acc):
    for slot, pair in enumerate(pairs):
        rows = slice(pair * ROWS, (pair + 1) * ROWS)
        pieces = []
        for z in range(NZ):
            a, b = own[z, rows, :], other[z, rows, :]
            pieces += [jnp.where(scalars[5, 0] == 0, a, b), jnp.where(scalars[5, 0] == 0, b, a)]
        vh, vl = split(jnp.concatenate(pieces, axis=0))
        for term in range(4):
            lh, ll, rh, rl = parts(slot, pair, term)
            uh, ul = split(dot(lh, vh, NN) + dot(lh, vl, NN) + dot(ll, vh, NN))
            acc[pair + 1 + scalars[4, term]] += dot(uh, rh, NT) + dot(uh, rl, NT) + dot(ul, rh, NT)


def kept_parts(left, right):
    return lambda slot, pair, term: (left[0, term, slot], left[1, term, slot], right[0, term, slot], right[1, term, slot])


EDGES, INNER = (0, 3), (1, 2)


def copies_of(pairs, left, right, blocks, semaphores):
    return [
        pltpu.make_async_copy(
            operator.at[term, pairs[slot]], blocks.at[side, term, slot], semaphores.at[side, term, slot]
        )
        for slot in range(2)
        for term in range(4)
        for side, operator in enumerate((left, right))
    ]


def fresh_parts(scalars, blocks, left_parts, right_parts):
    def parts(slot, pair, term):
        active = (scalars[term, pair] > 0).astype(F32)
        lh, ll = split(blocks[0, term, slot] * active)
        rh, rl = split(blocks[1, term, slot])
        left_parts[0, term, slot], left_parts[1, term, slot] = lh, ll
        right_parts[0, term, slot], right_parts[1, term, slot] = rh, rl
        return lh, ll, rh, rl

    return parts


def parts_kernel(pairs, scalars, left, right, *rest):
    *_, left_parts, right_parts, blocks, semaphores = rest
    copies = copies_of(pairs, left, right, blocks, semaphores)
    for copy in copies:
        copy.start()
    parts = fresh_parts(scalars, blocks, left_parts, right_parts)
    for i, (slot, term) in enumerate((slot, term) for slot in range(2) for term in range(4)):
        copies[2 * i].wait()
        copies[2 * i + 1].wait()
        parts(slot, pairs[slot], term)


def edges_of(acc, scalars, kept, given):
    kept[...] = acc[5 * scalars[5, 0]]
    given[...] = acc[5 - 5 * scalars[5, 0]]


def edge_kernel(scalars, left_parts, right_parts, own, other, acc, kept, given, *totals):
    acc[...] = jnp.zeros_like(acc)
    items(EDGES, scalars, kept_parts(left_parts, right_parts), own, other, acc)
    edges_of(acc, scalars, kept, given)
    if totals:
        totals[0][...] = added(own[:, 64:72, :]) + added(other[:, 64:72, :])


def inner_kernel(scalars, left_parts, right_parts, own, other, start, acc):
    del start
    items(INNER, scalars, kept_parts(left_parts, right_parts), own, other, acc)


ACC, BLOCK = shape(6, BLK, BLK), shape(BLK, BLK)
BLOCKS = (2, 4, 2, BLK, BLK)
PARTS = shape(*BLOCKS, dtype=BF16)
COPIES = pltpu.SemaphoreType.DMA((2, 4, 2))


def on_blocks(kernel, outs, scalars, hbm, vmem, scratch=(), alias=None, flops=8 * 6 * 2 * BLK**3):
    return pl.pallas_call(
        kernel,
        in_specs=[SMEM] + [pl.BlockSpec(memory_space=pltpu.HBM)] * len(hbm) + [VMEM] * len(vmem),
        out_specs=[VMEM] * len(outs),
        out_shape=outs,
        scratch_shapes=scratch,
        input_output_aliases=alias or {},
        compiler_params=PARAMS,
        cost_estimate=pl.CostEstimate(flops=flops, bytes_accessed=8 * 2**19, transcendentals=0),
    )(scalars, *hbm, *vmem)


def arrange_kernel(scalars, acc, edge, *rest):
    *vectors, mine, theirs = rest
    from_low = (scalars[5, 0] == 1) & (scalars[5, 1] > 0)
    from_high = (scalars[5, 0] == 0) & (scalars[5, 1] < 15)
    dots = jnp.zeros((8, BLK), F32)
    norms = jnp.zeros((8, BLK), F32)
    for pair in range(4):
        for z in range(NZ):
            pieces = []
            for half in range(2):
                rows = slice((2 * z + half) * ROWS, (2 * z + half + 1) * ROWS)
                piece = acc[pair + 1, rows, :]
                if pair == 0:
                    piece = piece + jnp.where(from_low, edge[rows, :], 0.0)
                if pair == 3:
                    piece = piece + jnp.where(from_high, edge[rows, :], 0.0)
                pieces.append(piece)
            place = slice(pair * ROWS, (pair + 1) * ROWS)
            a = jnp.where(scalars[5, 0] == 0, pieces[0], pieces[1])
            b = jnp.where(scalars[5, 0] == 0, pieces[1], pieces[0])
            mine[z, place, :] = a
            theirs[z, place, :] = b
            if vectors:
                va, vb = vectors[0][z, place, :], vectors[1][z, place, :]
                d = a * va + b * vb
                n = va * va + vb * vb
                dots += d[:8] + d[8:]
                norms += n[:8] + n[8:]
    if vectors:
        row = lax.broadcasted_iota(jnp.int32, (8, BLK), 0)
        sums = jnp.where(row == 0, jnp.sum(dots), 0.0) + jnp.where(row == 1, jnp.sum(norms) * (1.0 / 16), 0.0)
        for z in range(NZ):
            mine[z, 64:72, :] = sums
            theirs[z, 64:72, :] = sums


def arrange(scalars, acc, edge, *vectors):
    return pl.pallas_call(
        arrange_kernel,
        in_specs=[SMEM] + [VMEM] * (2 + len(vectors)),
        out_specs=[VMEM, VMEM],
        out_shape=[shape(NZ, 72 if vectors else 64, BLK)] * 2,
        compiler_params=PARAMS,
    )(scalars, acc, edge, *vectors)


def added(parts):
    total = parts[0]
    for z in range(1, NZ):
        total += parts[z]
    return total


def image_kernel(parts, vector, weights, image, sums):
    total = added(parts)
    correlation, norm = total[64:65, 0:1], total[65:66, 0:1]
    usable = norm > 1e-18
    near = jnp.where(usable, correlation, 0.0) / jnp.where(usable, norm, 1.0)
    image[...] = total[:64]
    rest = (total[:64] - near * vector[...]) / weights[...]
    weighted = vector[...] / weights[...]
    products = (vector[...] * rest, vector[...] * weighted, rest * rest, rest * weighted, weighted * weighted)
    values = [correlation, norm, *(jnp.sum(x, keepdims=True) for x in products), near]
    row = lax.broadcasted_iota(jnp.int32, (8, 128), 0)
    rows = jnp.zeros((8, 128), F32)
    for i, value in enumerate(values):
        rows = jnp.where(row == i, value, rows)
    for i in range(16):
        sums[i] = rows


def scaled_kernel(parts, image, vector, weights, scaled, norm, sent):
    columns = [parts[i] for i in range(16)]
    correlation = sum((x[0:1] for x in columns[1:]), columns[0][0:1])
    total = sum((x[1:2] for x in columns[1:]), columns[0][1:2])
    rayleigh = correlation / total
    along = jnp.zeros((1, 128), F32)
    squares = jnp.zeros((1, 128), F32)
    for x in columns:
        change = rayleigh - x[7:8]
        along += x[2:3] - change * x[3:4]
        squares += x[4:5] - change * (2.0 * x[5:6] - change * x[6:7])
    norm[...] = jnp.broadcast_to(total[:, 0:1], (8, BLK))
    value = (image[...] - rayleigh[:, 0:1] * vector[...]) / weights[...]
    scaled[...] = value
    row = lax.broadcasted_iota(jnp.int32, (8, BLK), 0)
    rows = jnp.where(row == 0, along[:, 0:1], squares[:, 0:1])
    for z in range(NZ):
        sent[z, :64, :] = value
        sent[z, 64:72, :] = rows


def finish_kernel(entries, parts, image, vector, scaled, norm, totals, correction, image_new):
    projection, squares = totals[0:1, 0:1], totals[1:2, 0:1]
    along = projection / norm[0:1, 0:1]
    squares = jnp.maximum(squares - along * projection, 0.0)
    size = jnp.sqrt(squares / entries + EPSILON)
    correction[...] = (scaled[...] - along * vector[...]) / size
    image_new[...] = (added(parts) - along * image[...]) / size


def local(kernel, outs, *args):
    return pl.pallas_call(
        kernel, in_specs=[VMEM] * len(args), out_specs=[VMEM] * len(outs), out_shape=outs, compiler_params=PARAMS
    )(*args)


SWAP = [(i, i ^ 1) for i in range(16)]
SAME_CORE = [[2 * z + c for z in range(NZ)] for c in range(2)]
TO_EDGES = [(o * 16 + s, o * 16 + (s + 2 * (o % 2) - 1) % 16) for o in range(16) for s in range(16)]


def exchange(parts):
    return lax.all_to_all(parts, "ops", 0, 0, axis_index_groups=SAME_CORE)


def on_device(wavefunction, left_operators, right_operators, preconditioner, charges, coupling):
    entries = wavefunction.size * lax.axis_size("ops") * lax.axis_size("sec")
    core, position = lax.axis_index("ops") % 2, lax.axis_index("sec")
    place = jnp.where(jnp.arange(4) == 0, core, position).astype(jnp.int32)
    scalars = jnp.concatenate([coupling, charges[None], place[None]])
    slab = wavefunction.reshape(64, BLK)
    weights = preconditioner.reshape(64, BLK)
    slab, scalars = lax.optimization_barrier((slab, scalars))
    operators = [pltpu.with_memory_space_constraint(x, pltpu.HBM) for x in (left_operators, right_operators)]

    def combined(acc, edge, *vectors):
        mine, theirs = arrange(scalars, acc, edge, *vectors)
        return exchange(mine + lax.ppermute(theirs, "ops", SWAP))

    def to_neighbour(kept, given):
        return lax.ppermute(kept + lax.ppermute(given, "ops", SWAP), ("ops", "sec"), TO_EDGES)

    own = exchange(jnp.broadcast_to(slab[None], (NZ, 64, BLK)))
    other = lax.ppermute(own, "ops", SWAP)
    scratch = [pltpu.VMEM(BLOCKS, F32), COPIES]
    split_edges, split_inner = (functools.partial(parts_kernel, pairs) for pairs in (EDGES, INNER))
    edge_parts = on_blocks(split_edges, [PARTS] * 2, scalars, operators, [], scratch, flops=0)
    acc, kept, given = on_blocks(edge_kernel, [ACC, BLOCK, BLOCK], scalars, [], [*edge_parts, own, other])
    edge = to_neighbour(kept, given)
    inner_parts = on_blocks(split_inner, [PARTS] * 2, scalars, operators, [], scratch, flops=0)
    (acc,) = on_blocks(inner_kernel, [ACC], scalars, [], [*inner_parts, own, other, acc], alias={5: 0})
    parts = combined(acc, edge, own, other)

    image, sums = local(image_kernel, [shape(64, BLK), shape(16, 8, 128)], parts, slab, weights)
    sums = lax.all_to_all(sums, "sec", 0, 0)
    outs = [shape(64, BLK), shape(8, BLK), shape(NZ, 72, BLK)]
    scaled, norm, sent = local(scaled_kernel, outs, sums, image, slab, weights)

    own = exchange(sent)
    other = lax.ppermute(own, "ops", SWAP)
    outs = [ACC, BLOCK, BLOCK, shape(8, BLK)]
    acc, kept, given, totals = on_blocks(edge_kernel, outs, scalars, [], [*edge_parts, own, other])
    edge = to_neighbour(kept, given)
    (acc,) = on_blocks(inner_kernel, [ACC], scalars, [], [*inner_parts, own, other, acc], alias={5: 0})
    parts = combined(acc, edge)
    finish = functools.partial(finish_kernel, float(entries))
    correction, image_new = local(finish, [shape(64, BLK)] * 2, parts, image, slab, scaled, norm, totals)
    return correction.reshape(wavefunction.shape), image_new.reshape(wavefunction.shape)


def solution(mesh):
    placed = (
        P("sec", "ops", None),
        P("ops", "sec", None, None),
        P("ops", "sec", None, None),
        P("sec", "ops", None),
        P("ops"),
        P("ops", "sec"),
    )
    return jax.shard_map(
        on_device,
        mesh=mesh,
        in_specs=placed,
        out_specs=(P("sec", "ops", None), P("sec", "ops", None)),
        check_vma=False,
    )
```

time: 150 us -> 146 us (0.973)
  starting transfers between devices: 16 us -> 11.6 us
  blocking collectives: 99.6 us -> 96.6 us
  waiting for transfers between devices: 12.7 us -> 15 us
  Pallas kernels: 18.3 us -> 19.8 us
    ppermute x1 -> x0, starting transfers between devices: 6.21 us -> none  [on_device(): totals = lax.ppermute(totals, ('ops', 'sec'), DIAGONAL)]
    ppermute x2, waiting for transfers between devices: 4.72 us -> 7.14 us  [to_neighbour(): lax.ppermute(kept + lax.ppermute(given, 'ops', SWAP), ('ops', 'sec'), TO_...]
    all_to_all x1, blocking collectives: 13.2 us -> 11.4 us  [on_device(): sums = lax.all_to_all(sums, 'sec', 0, 0)]
    ppermute x2, starting transfers between devices: 0.73 us -> 2.53 us  [combined(): return exchange(mine + lax.ppermute(theirs, 'ops', SWAP))]
    pallas_call x5 -> x6, Pallas kernels: 15.8 us -> 17 us  [on_blocks(): pl.pallas_call(kernel, in_specs=[SMEM] + [pl.BlockSpec(memory_space=pltpu...]
  transfers between devices with their start and end apart: 9 -> 8, of which waited for: 6 -> 7; matrix products, arithmetic and copies ran while one was open for 0% -> 0% of each run, Pallas kernels for 6% -> 8%
where the time goes in v3:
time: 146 us
  blocking collectives  96.6 us (66%)
  Pallas kernels  19.8 us (14%)
  waiting for transfers between devices  15 us (10%)
  starting transfers between devices  11.6 us (8%)
    all_to_all x4, blocking collectives, exchange(): return lax.all_to_all(parts, 'ops', 0, 0, axis_index_groups=SAME_CORE)  85.2 us
    pallas_call x6, Pallas kernels, on_blocks(): pl.pallas_call(kernel, in_specs=[SMEM] + [pl.BlockSpec(memory_space=pltpu...  17 us
    all_to_all x1, blocking collectives, on_device(): sums = lax.all_to_all(sums, 'sec', 0, 0)  11.4 us
    ppermute x2, waiting for transfers between devices, to_neighbour(): lax.ppermute(kept + lax.ppermute(given, 'ops', SWAP), ('ops', 'sec'), TO_...  7.14 us
    ppermute x2, starting transfers between devices, on_device(): other = lax.ppermute(own, 'ops', SWAP)  6.45 us
    ppermute x2, waiting for transfers between devices, combined(): return exchange(mine + lax.ppermute(theirs, 'ops', SWAP))  3.53 us
  transfers between devices with their start and end apart: 8, of which 7 were waited for; matrix products, arithmetic and copies ran while one was open for 0% of the time, Pallas kernels for 8%

profile of v3, /device:TPU:1, one launch (start us, length us, event | category | flops | bytes accessed | tf_op | source)
XLA Modules:
  0.0 145.6 jit_solution(13761771938292749693)
XLA Ops:
  0.7 0.7 pad_add_fusion.scalars
  1.4 0.9 broadcast_in_dim.21
  2.2 24.8 %all_to_all.25.own.rest_0_ = f32[8,64,256]{2,1,0:T(8,128)S(1)} all-to-all(f32[8,64,256]{2,1,0:T(8,128)S(1)} %broadcast_in_dim.21), channel_id=1, replica_groups={{0,32,64,96,128,160,192,224},{16,48,80,112,144,176,208,240},{1,33,65,97..., dimensions={0} | all-to-all | bytes 1048576 | tf_op jit(solution)/shard_map/all_to_all | solution.py:242
  27.1 2.5 %collective-permute-start = (f32[8,64,256]{2,1,0:T(8,128)S(1)}, f32[8,64,256]{2,1,0:T(8,128)S(1)}, u32[]{:S(2)}, u32[]{:S(2)}) collective-permute-start(f32[8,64,256]{2,1,0:T(8,128)S(1)} %all_to_all.25.own.rest_0_), channel_id=1, source_target_pairs={{0,16},{16,0},{32,48},{48,32},{64,80},{80,64},{96,112},{112,96},{1... | collective-permute-start | bytes 1572872 | tf_op jit(solution)/shard_map/ppermute | solution.py:263
  29.5 3.0 %shard_map.78 = (bf16[2,4,2,256,256]{4,3,2,1,0:T(8,128)(2,1)S(1)}, bf16[2,4,2,256,256]{4,3,2,1,0:T(8,128)(2,1)S(1)}) custom-call(s32[6,4]{1,0:T(8,128)S(1)} %pad_add_fusion.scalars, f32[4,4,256,256]{3,2,1,0:T(8,128)} %left.3, f32[4,4,256,256]{3,2,1,0:T(8,128)} %right.3), custom_call_target="tpu_custom_call" | custom-call | bytes 4194304 | tf_op jit(solution)/shard_map/pallas_call | solution.py:117
  32.5 0.0 collective-permute-done.other.rest_1_
  32.5 2.8 %shard_map.79 = (f32[6,256,256]{2,1,0:T(8,128)S(1)}, f32[256,256]{1,0:T(8,128)S(1)}, f32[256,256]{1,0:T(8,128)S(1)}) custom-call(s32[6,4]{1,0:T(8,128)S(1)} %pad_add_fusion.scalars, bf16[2,4,2,256,256]{4,3,2,1,0:T(8,128)(2,1)S(1)} %get-tuple-element.30.left_parts, bf16[2,4,2,256,256]{4,3,2,1,0:T(8,128)(2,1)S(1)} %get-tuple-element.31.right_parts, ...), custom_call_target="tpu_custom_call" | custom-call | flops 1610612736 | bytes 4194304 | tf_op jit(solution)/shard_map/pallas_call | solution.py:117
  35.3 0.1 collective-permute-start.1
  35.4 1.5 %collective-permute-done.1 = f32[256,256]{1,0:T(8,128)S(1)} collective-permute-done((f32[256,256]{1,0:T(8,128)S(1)}, f32[256,256]{1,0:T(8,128)S(1)}, u32[]{:S(2)}, u32[]{:S(2)}) %collective-permute-start.1) | collective-permute-done | bytes 262176 | tf_op jit(solution)/shard_map/ppermute | solution.py:260
  37.0 1.3 collective-permute-start.2
  38.3 3.0 %shard_map.77 = (bf16[2,4,2,256,256]{4,3,2,1,0:T(8,128)(2,1)S(1)}, bf16[2,4,2,256,256]{4,3,2,1,0:T(8,128)(2,1)S(1)}) custom-call(s32[6,4]{1,0:T(8,128)S(1)} %pad_add_fusion.scalars, f32[4,4,256,256]{3,2,1,0:T(8,128)} %left.3, f32[4,4,256,256]{3,2,1,0:T(8,128)} %right.3), custom_call_target="tpu_custom_call" | custom-call | bytes 4194304 | tf_op jit(solution)/shard_map/pallas_call | solution.py:117
  41.3 2.7 %shard_map.80.acc = f32[6,256,256]{2,1,0:T(8,128)S(1)} custom-call(s32[6,4]{1,0:T(8,128)S(1)} %pad_add_fusion.scalars, bf16[2,4,2,256,256]{4,3,2,1,0:T(8,128)(2,1)S(1)} %get-tuple-element.27.left_parts, bf16[2,4,2,256,256]{4,3,2,1,0:T(8,128)(2,1)S(1)} %get-tuple-element.28.right_parts, ...), custom_call_target="tpu_custom_call", output_to_operand_aliasing={{}: (5, {})} | custom-call | flops 1610612736 | bytes 4194304 | tf_op jit(solution)/shard_map/pallas_call | solution.py:117
  44.0 1.8 %collective-permute-done.2.edge = f32[256,256]{1,0:T(8,128)S(1)} collective-permute-done((f32[256,256]{1,0:T(8,128)S(1)}, f32[256,256]{1,0:T(8,128)S(1)}, u32[]{:S(2)}, u32[]{:S(2)}) %collective-permute-start.2) | collective-permute-done | bytes 262176 | tf_op jit(solution)/shard_map/ppermute | solution.py:260
  45.8 1.0 shard_map.81
  46.8 0.0 copy-start
  46.8 0.0 copy-start.1
  46.8 2.4 %collective-permute-start.3 = (f32[8,72,256]{2,1,0:T(8,128)S(1)}, f32[8,72,256]{2,1,0:T(8,128)S(1)}, u32[]{:S(2)}, u32[]{:S(2)}) collective-permute-start(f32[8,72,256]{2,1,0:T(8,128)S(1)} %get-tuple-element.36), channel_id=1, source_target_pairs={{0,16},{16,0},{32,48},{48,32},{64,80},{80,64},{96,112},{112,96},{1... | collective-permute-start | bytes 1769480 | tf_op jit(solution)/shard_map/ppermute | solution.py:257
  49.2 1.6 %collective-permute-done.3 = f32[8,72,256]{2,1,0:T(8,128)S(1)} collective-permute-done((f32[8,72,256]{2,1,0:T(8,128)S(1)}, f32[8,72,256]{2,1,0:T(8,128)S(1)}, u32[]{:S(2)}, u32[]{:S(2)}) %collective-permute-start.3) | collective-permute-done | bytes 589856 | tf_op jit(solution)/shard_map/ppermute | solution.py:257
  50.9 0.1 add.18
  50.9 21.8 %all_to_all.26.parts = f32[8,72,256]{2,1,0:T(8,128)S(1)} all-to-all(f32[8,72,256]{2,1,0:T(8,128)S(1)} %add.18), channel_id=1, replica_groups={{0,32,64,96,128,160,192,224},{16,48,80,112,144,176,208,240},{1,33,65,97..., dimensions={0} | all-to-all | bytes 1179648 | tf_op jit(solution)/shard_map/all_to_all | solution.py:242
  72.7 0.0 copy-done
  72.7 0.0 copy-done.1
  72.7 0.2 shard_map.82
  72.9 11.4 %all_to_all.27.parts = f32[16,8,128]{2,1,0:T(8,128)S(1)} all-to-all(f32[16,8,128]{2,1,0:T(8,128)S(1)} %get-tuple-element.37), channel_id=1, replica_groups=mesh['ops'=16,'sec'=16] {'sec'}, dimensions={0} | all-to-all | bytes 131072 | tf_op jit(solution)/shard_map/all_to_all | solution.py:274
  84.3 0.1 shard_map.83
  84.4 18.2 %all_to_all.28.own = f32[8,72,256]{2,1,0:T(8,128)S(1)} all-to-all(f32[8,72,256]{2,1,0:T(8,128)S(1)} %get-tuple-element.39), channel_id=1, replica_groups={{0,32,64,96,128,160,192,224},{16,48,80,112,144,176,208,240},{1,33,65,97..., dimensions={0} | all-to-all | bytes 1179648 | tf_op jit(solution)/shard_map/all_to_all | solution.py:242
  102.7 4.0 %collective-permute-start.4 = (f32[8,72,256]{2,1,0:T(8,128)S(1)}, f32[8,72,256]{2,1,0:T(8,128)S(1)}, u32[]{:S(2)}, u32[]{:S(2)}) collective-permute-start(f32[8,72,256]{2,1,0:T(8,128)S(1)} %all_to_all.28.own), channel_id=1, source_target_pairs={{0,16},{16,0},{32,48},{48,32},{64,80},{80,64},{96,112},{112,96},{1... | collective-permute-start | bytes 1769480 | tf_op jit(solution)/shard_map/ppermute | solution.py:279
  106.7 1.6 %collective-permute-done.4.other = f32[8,72,256]{2,1,0:T(8,128)S(1)} collective-permute-done((f32[8,72,256]{2,1,0:T(8,128)S(1)}, f32[8,72,256]{2,1,0:T(8,128)S(1)}, u32[]{:S(2)}, u32[]{:S(2)}) %collective-permute-start.4) | collective-permute-done | bytes 589856 | tf_op jit(solution)/shard_map/ppermute | solution.py:279
  108.3 2.8 %shard_map.84 = (f32[6,256,256]{2,1,0:T(8,128)S(1)}, f32[256,256]{1,0:T(8,128)S(1)}, f32[256,256]{1,0:T(8,128)S(1)}, f32[8,256]{1,0:T(8,128)S(1)}) custom-call(s32[6,4]{1,0:T(8,128)S(1)} %pad_add_fusion.scalars, bf16[2,4,2,256,256]{4,3,2,1,0:T(8,128)(2,1)S(1)} %get-tuple-element.30.left_parts, ...), custom_call_target="tpu_custom_call" | custom-call | flops 1610612736 | bytes 4194304 | tf_op jit(solution)/shard_map/pallas_call | solution.py:117
  111.2 0.6 collective-permute-start.5
  111.8 1.2 collective-permute-done.5
  113.0 0.6 collective-permute-start.6
  113.6 2.7 %shard_map.85.acc = f32[6,256,256]{2,1,0:T(8,128)S(1)} custom-call(s32[6,4]{1,0:T(8,128)S(1)} %pad_add_fusion.scalars, bf16[2,4,2,256,256]{4,3,2,1,0:T(8,128)(2,1)S(1)} %get-tuple-element.27.left_parts, bf16[2,4,2,256,256]{4,3,2,1,0:T(8,128)(2,1)S(1)} %get-tuple-element.28.right_parts, ...), custom_call_target="tpu_custom_call", output_to_operand_aliasing={{}: (5, {})} | custom-call | flops 1610612736 | bytes 4194304 | tf_op jit(solution)/shard_map/pallas_call | solution.py:117
  116.3 5.4 %collective-permute-done.6.edge = f32[256,256]{1,0:T(8,128)S(1)} collective-permute-done((f32[256,256]{1,0:T(8,128)S(1)}, f32[256,256]{1,0:T(8,128)S(1)}, u32[]{:S(2)}, u32[]{:S(2)}) %collective-permute-start.6) | collective-permute-done | bytes 262176 | tf_op jit(solution)/shard_map/ppermute | solution.py:260
  121.6 0.7 shard_map.86
  122.3 0.1 collective-permute-start.7
  122.4 1.9 %collective-permute-done.7 = f32[8,64,256]{2,1,0:T(8,128)S(1)} collective-permute-done((f32[8,64,256]{2,1,0:T(8,128)S(1)}, f32[8,64,256]{2,1,0:T(8,128)S(1)}, u32[]{:S(2)}, u32[]{:S(2)}) %collective-permute-start.7) | collective-permute-done | bytes 524320 | tf_op jit(solution)/shard_map/ppermute | solution.py:257
  124.3 0.1 add.20
  124.4 20.4 %all_to_all.29.parts = f32[8,64,256]{2,1,0:T(8,128)S(1)} all-to-all(f32[8,64,256]{2,1,0:T(8,128)S(1)} %add.20), channel_id=1, replica_groups={{0,32,64,96,128,160,192,224},{16,48,80,112,144,176,208,240},{1,33,65,97..., dimensions={0} | all-to-all | bytes 1048576 | tf_op jit(solution)/shard_map/all_to_all | solution.py:242
  144.8 0.8 shard_map.87
  (3 shorter events, 0.1 us)
Async XLA Ops:
  27.1 5.4 %collective-permute-start = (f32[8,64,256]{2,1,0:T(8,128)S(1)}, f32[8,64,256]{2,1,0:T(8,128)S(1)}, u32[]{:S(2)}, u32[]{:S(2)}) collective-permute-start(f32[8,64,256]{2,1,0:T(8,128)S(1)} %all_to_all.25.own.rest_0_), channel_id=1, source_target_pairs={{0,16},{16,0},{32,48},{48,32},{64,80},{80,64},{96,112},{112,96},{1... | collective-permute-start | bytes 1572872 | tf_op jit(solution)/shard_map/ppermute | solution.py:263
  35.3 1.6 %collective-permute-start.1 = (f32[256,256]{1,0:T(8,128)S(1)}, f32[256,256]{1,0:T(8,128)S(1)}, u32[]{:S(2)}, u32[]{:S(2)}) collective-permute-start(f32[256,256]{1,0:T(8,128)S(1)} %get-tuple-element.34), channel_id=1, source_target_pairs={{0,16},{16,0},{32,48},{48,32},{64,80},{80,64},{96,112},{112,96},{1... | collective-permute-start | bytes 786440 | tf_op jit(solution)/shard_map/ppermute | solution.py:260
  37.0 8.8 %collective-permute-start.2 = (f32[256,256]{1,0:T(8,128)S(1)}, f32[256,256]{1,0:T(8,128)S(1)}, u32[]{:S(2)}, u32[]{:S(2)}) collective-permute-start(f32[256,256]{1,0:T(8,128)S(1)} %add.17), channel_id=1, source_target_pairs={{0,15},{1,0},{2,1},{3,2},{4,3},{5,4},{6,5},{7,6},{8,7},{9,8},{10,9... | collective-permute-start | bytes 786440 | tf_op jit(solution)/shard_map/ppermute | solution.py:260
  46.8 25.9 %copy-start = (f32[4,16,256]{2,1,0:T(8,128)S(1)}, f32[4,16,256]{2,1,0:T(8,128)}, u32[]{:S(2)}) copy-start(f32[4,16,256]{2,1,0:T(8,128)} %param.6) | copy-start | bytes 196612
  46.8 25.9 %copy-start.1 = (f32[4,16,256]{2,1,0:T(8,128)S(1)}, f32[4,16,256]{2,1,0:T(8,128)}, u32[]{:S(2)}) copy-start(f32[4,16,256]{2,1,0:T(8,128)} %param.9) | copy-start | bytes 196612
  46.8 4.1 %collective-permute-start.3 = (f32[8,72,256]{2,1,0:T(8,128)S(1)}, f32[8,72,256]{2,1,0:T(8,128)S(1)}, u32[]{:S(2)}, u32[]{:S(2)}) collective-permute-start(f32[8,72,256]{2,1,0:T(8,128)S(1)} %get-tuple-element.36), channel_id=1, source_target_pairs={{0,16},{16,0},{32,48},{48,32},{64,80},{80,64},{96,112},{112,96},{1... | collective-permute-start | bytes 1769480 | tf_op jit(solution)/shard_map/ppermute | solution.py:257
  102.7 5.6 %collective-permute-start.4 = (f32[8,72,256]{2,1,0:T(8,128)S(1)}, f32[8,72,256]{2,1,0:T(8,128)S(1)}, u32[]{:S(2)}, u32[]{:S(2)}) collective-permute-start(f32[8,72,256]{2,1,0:T(8,128)S(1)} %all_to_all.28.own), channel_id=1, source_target_pairs={{0,16},{16,0},{32,48},{48,32},{64,80},{80,64},{96,112},{112,96},{1... | collective-permute-start | bytes 1769480 | tf_op jit(solution)/shard_map/ppermute | solution.py:279
  111.2 1.8 %collective-permute-start.5 = (f32[256,256]{1,0:T(8,128)S(1)}, f32[256,256]{1,0:T(8,128)S(1)}, u32[]{:S(2)}, u32[]{:S(2)}) collective-permute-start(f32[256,256]{1,0:T(8,128)S(1)} %get-tuple-element.42), channel_id=1, source_target_pairs={{0,16},{16,0},{32,48},{48,32},{64,80},{80,64},{96,112},{112,96},{1... | collective-permute-start | bytes 786440 | tf_op jit(solution)/shard_map/ppermute | solution.py:260
  113.0 8.6 %collective-permute-start.6 = (f32[256,256]{1,0:T(8,128)S(1)}, f32[256,256]{1,0:T(8,128)S(1)}, u32[]{:S(2)}, u32[]{:S(2)}) collective-permute-start(f32[256,256]{1,0:T(8,128)S(1)} %add.19), channel_id=1, source_target_pairs={{0,15},{1,0},{2,1},{3,2},{4,3},{5,4},{6,5},{7,6},{8,7},{9,8},{10,9... | collective-permute-start | bytes 786440 | tf_op jit(solution)/shard_map/ppermute | solution.py:260
  122.3 2.0 %collective-permute-start.7 = (f32[8,64,256]{2,1,0:T(8,128)S(1)}, f32[8,64,256]{2,1,0:T(8,128)S(1)}, u32[]{:S(2)}, u32[]{:S(2)}) collective-permute-start(f32[8,64,256]{2,1,0:T(8,128)S(1)} %get-tuple-element.44), channel_id=1, source_target_pairs={{0,16},{16,0},{32,48},{48,32},{64,80},{80,64},{96,112},{112,96},{1... | collective-permute-start | bytes 1572872 | tf_op jit(solution)/shard_map/ppermute | solution.py:257

commit v4 on v3

--- a/solution.py
+++ b/solution.py
@@ -94,17 +94,49 @@
     given[...] = acc[5 - 5 * scalars[5, 0]]
 
 
-def edge_kernel(scalars, left_parts, right_parts, own, other, acc, kept, given, *totals):
+def edge_kernel(scalars, left_parts, right_parts, own, other, acc, kept, given):
     acc[...] = jnp.zeros_like(acc)
     items(EDGES, scalars, kept_parts(left_parts, right_parts), own, other, acc)
     edges_of(acc, scalars, kept, given)
-    if totals:
-        totals[0][...] = added(own[:, 64:72, :]) + added(other[:, 64:72, :])
+
+
+def rows_of(z, half):
+    return pl.ds(pl.multiple_of((2 * z + half) * ROWS, ROWS), ROWS)
+
+
+def last_edge_kernel(scalars, left_parts, right_parts, own, other, acc, low, high, given, totals):
+    acc[...] = jnp.zeros_like(acc)
+    items(EDGES, scalars, kept_parts(left_parts, right_parts), own, other, acc)
+    core = scalars[5, 0]
+    for z in range(NZ):
+        low[z] = acc[0, rows_of(z, core), :]
+        high[z] = acc[5, rows_of(z, core), :]
+        given[0, z] = acc[0, rows_of(z, 1 - core), :]
+        given[1, z] = acc[5, rows_of(z, 1 - core), :]
+    totals[...] = added(own[:, 64:72, :]) + added(other[:, 64:72, :])
 
 
 def inner_kernel(scalars, left_parts, right_parts, own, other, start, acc):
     del start
     items(INNER, scalars, kept_parts(left_parts, right_parts), own, other, acc)
+
+
+def last_inner_kernel(scalars, left_parts, right_parts, own, other, start, acc, mine, theirs):
+    del start
+    items(INNER, scalars, kept_parts(left_parts, right_parts), own, other, acc)
+    core = scalars[5, 0]
+    for z in range(NZ):
+        for pair in range(4):
+            place = slice(pair * ROWS, (pair + 1) * ROWS)
+            mine[z, place, :] = acc[pair + 1, rows_of(z, core), :]
+            theirs[z, place, :] = acc[pair + 1, rows_of(z, 1 - core), :]
+
+
+def last_sums_kernel(scalars, mine, theirs, from_low, from_high, sent):
+    low, high = scalars[5, 1] > 0, scalars[5, 1] < 15
+    sent[:, :16, :] = mine[:, :16, :] + theirs[:, :16, :] + jnp.where(low, from_low[...], 0.0)
+    sent[:, 16:48, :] = mine[:, 16:48, :] + theirs[:, 16:48, :]
+    sent[:, 48:, :] = mine[:, 48:, :] + theirs[:, 48:, :] + jnp.where(high, from_high[...], 0.0)
 
 
 ACC, BLOCK = shape(6, BLK, BLK), shape(BLK, BLK)
@@ -126,8 +158,7 @@
     )(scalars, *hbm, *vmem)
 
 
-def arrange_kernel(scalars, acc, edge, *rest):
-    *vectors, mine, theirs = rest
+def arrange_kernel(scalars, acc, edge, own, other, mine, theirs):
     from_low = (scalars[5, 0] == 1) & (scalars[5, 1] > 0)
     from_high = (scalars[5, 0] == 0) & (scalars[5, 1] < 15)
     dots = jnp.zeros((8, BLK), F32)
@@ -148,28 +179,16 @@
             b = jnp.where(scalars[5, 0] == 0, pieces[1], pieces[0])
             mine[z, place, :] = a
             theirs[z, place, :] = b
-            if vectors:
-                va, vb = vectors[0][z, place, :], vectors[1][z, place, :]
-                d = a * va + b * vb
-                n = va * va + vb * vb
-                dots += d[:8] + d[8:]
-                norms += n[:8] + n[8:]
-    if vectors:
-        row = lax.broadcasted_iota(jnp.int32, (8, BLK), 0)
-        sums = jnp.where(row == 0, jnp.sum(dots), 0.0) + jnp.where(row == 1, jnp.sum(norms) * (1.0 / 16), 0.0)
-        for z in range(NZ):
-            mine[z, 64:72, :] = sums
-            theirs[z, 64:72, :] = sums
-
-
-def arrange(scalars, acc, edge, *vectors):
-    return pl.pallas_call(
-        arrange_kernel,
-        in_specs=[SMEM] + [VMEM] * (2 + len(vectors)),
-        out_specs=[VMEM, VMEM],
-        out_shape=[shape(NZ, 72 if vectors else 64, BLK)] * 2,
-        compiler_params=PARAMS,
-    )(scalars, acc, edge, *vectors)
+            va, vb = own[z, place, :], other[z, place, :]
+            d = a * va + b * vb
+            n = va * va + vb * vb
+            dots += d[:8] + d[8:]
+            norms += n[:8] + n[8:]
+    row = lax.broadcasted_iota(jnp.int32, (8, BLK), 0)
+    sums = jnp.where(row == 0, jnp.sum(dots), 0.0) + jnp.where(row == 1, jnp.sum(norms) * (1.0 / 16), 0.0)
+    for z in range(NZ):
+        mine[z, 64:72, :] = sums
+        theirs[z, 64:72, :] = sums
 
 
 def added(parts):
@@ -233,6 +252,8 @@
     )(*args)
 
 
+UP = [(i, (i + 1) % 16) for i in range(16)]
+DOWN = [(i, (i - 1) % 16) for i in range(16)]
 SWAP = [(i, i ^ 1) for i in range(16)]
 SAME_CORE = [[2 * z + c for z in range(NZ)] for c in range(2)]
 TO_EDGES = [(o * 16 + s, o * 16 + (s + 2 * (o % 2) - 1) % 16) for o in range(16) for s in range(16)]
@@ -252,23 +273,21 @@
     slab, scalars = lax.optimization_barrier((slab, scalars))
     operators = [pltpu.with_memory_space_constraint(x, pltpu.HBM) for x in (left_operators, right_operators)]
 
-    def combined(acc, edge, *vectors):
-        mine, theirs = arrange(scalars, acc, edge, *vectors)
-        return exchange(mine + lax.ppermute(theirs, "ops", SWAP))
-
-    def to_neighbour(kept, given):
-        return lax.ppermute(kept + lax.ppermute(given, "ops", SWAP), ("ops", "sec"), TO_EDGES)
+    def swap(x):
+        return lax.ppermute(x, "ops", SWAP)
 
     own = exchange(jnp.broadcast_to(slab[None], (NZ, 64, BLK)))
-    other = lax.ppermute(own, "ops", SWAP)
+    other = swap(own)
     scratch = [pltpu.VMEM(BLOCKS, F32), COPIES]
     split_edges, split_inner = (functools.partial(parts_kernel, pairs) for pairs in (EDGES, INNER))
     edge_parts = on_blocks(split_edges, [PARTS] * 2, scalars, operators, [], scratch, flops=0)
     acc, kept, given = on_blocks(edge_kernel, [ACC, BLOCK, BLOCK], scalars, [], [*edge_parts, own, other])
-    edge = to_neighbour(kept, given)
+    edge = lax.ppermute(kept + swap(given), ("ops", "sec"), TO_EDGES)
     inner_parts = on_blocks(split_inner, [PARTS] * 2, scalars, operators, [], scratch, flops=0)
     (acc,) = on_blocks(inner_kernel, [ACC], scalars, [], [*inner_parts, own, other, acc], alias={5: 0})
-    parts = combined(acc, edge, own, other)
+    halves, vectors = [shape(NZ, 72, BLK)] * 2, [acc, edge, own, other]
+    mine, theirs = on_blocks(arrange_kernel, halves, scalars, [], vectors, flops=0)
+    parts = exchange(mine + swap(theirs))
 
     image, sums = local(image_kernel, [shape(64, BLK), shape(16, 8, 128)], parts, slab, weights)
     sums = lax.all_to_all(sums, "sec", 0, 0)
@@ -276,12 +295,18 @@
     scaled, norm, sent = local(scaled_kernel, outs, sums, image, slab, weights)
 
     own = exchange(sent)
-    other = lax.ppermute(own, "ops", SWAP)
-    outs = [ACC, BLOCK, BLOCK, shape(8, BLK)]
-    acc, kept, given, totals = on_blocks(edge_kernel, outs, scalars, [], [*edge_parts, own, other])
-    edge = to_neighbour(kept, given)
-    (acc,) = on_blocks(inner_kernel, [ACC], scalars, [], [*inner_parts, own, other, acc], alias={5: 0})
-    parts = combined(acc, edge)
+    other = swap(own)
+    strip = shape(NZ, ROWS, BLK)
+    outs = [ACC, strip, strip, shape(2, NZ, ROWS, BLK), shape(8, BLK)]
+    acc, low, high, given, totals = on_blocks(last_edge_kernel, outs, scalars, [], [*edge_parts, own, other])
+    given = swap(given)
+    from_high = lax.ppermute(low + given[0], "sec", DOWN)
+    from_low = lax.ppermute(high + given[1], "sec", UP)
+    outs, vectors = [ACC, *[shape(NZ, 64, BLK)] * 2], [*inner_parts, own, other, acc]
+    _, mine, theirs = on_blocks(last_inner_kernel, outs, scalars, [], vectors, alias={5: 0})
+    vectors = [mine, swap(theirs), from_low, from_high]
+    (sent,) = on_blocks(last_sums_kernel, [shape(NZ, 64, BLK)], scalars, [], vectors, flops=0)
+    parts = exchange(sent)
     finish = functools.partial(finish_kernel, float(entries))
     correction, image_new = local(finish, [shape(64, BLK)] * 2, parts, image, slab, scaled, norm, totals)
     return correction.reshape(wavefunction.shape), image_new.reshape(wavefunction.shape)

time: 146 us -> 144 us (0.986)
  blocking collectives: 96.6 us -> 93.9 us
    all_to_all x4, blocking collectives: 85.2 us -> 82.5 us  [exchange(): return lax.all_to_all(parts, 'ops', 0, 0, axis_index_groups=SAME_CORE)]
    pallas_call x2 -> x0, Pallas kernels: 1.68 us -> none  [arrange(): pl.pallas_call(arrange_kernel, in_specs=[SMEM] + [VMEM] * (2 + len(vector...]
    pallas_call x6 -> x8, Pallas kernels: 17 us -> 18.6 us  [on_blocks(): pl.pallas_call(kernel, in_specs=[SMEM] + [pl.BlockSpec(memory_space=pltpu...]
    ppermute x8 -> x9, starting transfers between devices: 11.6 us -> 12.7 us  [the longest x6 9.83 us: swap(): return lax.ppermute(x, 'ops', SWAP)]
    ppermute x8 -> x9, waiting for transfers between devices: 15 us -> 14.3 us  [the longest x6 4.79 us: swap(): return lax.ppermute(x, 'ops', SWAP)]
  transfers between devices with their start and end apart: 8 -> 9, of which waited for: 7 -> 6; matrix products, arithmetic and copies ran while one was open for 0% -> 0% of each run, Pallas kernels for 8% -> 8%
where the time goes in v4:
time: 144 us; the launch traced here: 143 us
  blocking collectives  93.9 us (65%)
  Pallas kernels  19.7 us (14%)
  waiting for transfers between devices  14.3 us (10%)
  starting transfers between devices  12.7 us (9%)
    all_to_all x4, blocking collectives, exchange(): return lax.all_to_all(parts, 'ops', 0, 0, axis_index_groups=SAME_CORE)  82.5 us
    pallas_call x8, Pallas kernels, on_blocks(): pl.pallas_call(kernel, in_specs=[SMEM] + [pl.BlockSpec(memory_space=pltpu...  18.6 us
    all_to_all x1, blocking collectives, on_device(): sums = lax.all_to_all(sums, 'sec', 0, 0)  11.4 us
    ppermute x6, starting transfers between devices, swap(): return lax.ppermute(x, 'ops', SWAP)  9.83 us
    ppermute x6, waiting for transfers between devices, swap(): return lax.ppermute(x, 'ops', SWAP)  4.79 us
    ppermute x1, waiting for transfers between devices, on_device(): from_low = lax.ppermute(high + given[1], 'sec', UP)  4.48 us
    ppermute x1, waiting for transfers between devices, on_device(): from_high = lax.ppermute(low + given[0], 'sec', DOWN)  3.22 us
  transfers between devices with their start and end apart: 9, of which 6 were waited for; matrix products, arithmetic and copies ran while one was open for 0% of the time, Pallas kernels for 8%

profile of v4, /device:TPU:1, one launch (start us, length us, event | category | flops | bytes accessed | tf_op | source)
XLA Modules:
  0.0 143.2 jit_solution(3248383663152144416)
XLA Ops:
  0.7 0.7 pad_add_fusion.scalars
  1.4 0.9 broadcast_in_dim.21
  2.2 24.8 %all_to_all.25.own = f32[8,64,256]{2,1,0:T(8,128)S(1)} all-to-all(f32[8,64,256]{2,1,0:T(8,128)S(1)} %broadcast_in_dim.21), channel_id=1, replica_groups={{0,32,64,96,128,160,192,224},{16,48,80,112,144,176,208,240},{1,33,65,97..., dimensions={0} | all-to-all | bytes 1048576 | tf_op jit(solution)/shard_map/all_to_all | solution.py:263
  27.1 2.5 %collective-permute-start = (f32[8,64,256]{2,1,0:T(8,128)S(1)}, f32[8,64,256]{2,1,0:T(8,128)S(1)}, u32[]{:S(2)}, u32[]{:S(2)}) collective-permute-start(f32[8,64,256]{2,1,0:T(8,128)S(1)} %all_to_all.25.own), channel_id=1, source_target_pairs={{0,16},{16,0},{32,48},{48,32},{64,80},{80,64},{96,112},{112,96},{1... | collective-permute-start | bytes 1572872 | tf_op jit(solution)/shard_map/ppermute | solution.py:277
  29.5 3.0 %shard_map.78 = (bf16[2,4,2,256,256]{4,3,2,1,0:T(8,128)(2,1)S(1)}, bf16[2,4,2,256,256]{4,3,2,1,0:T(8,128)(2,1)S(1)}) custom-call(s32[6,4]{1,0:T(8,128)S(1)} %pad_add_fusion.scalars, f32[4,4,256,256]{3,2,1,0:T(8,128)} %left.3, f32[4,4,256,256]{3,2,1,0:T(8,128)} %right.3), custom_call_target="tpu_custom_call" | custom-call | bytes 4194304 | tf_op jit(solution)/shard_map/pallas_call | solution.py:149
  32.5 0.0 collective-permute-done.other
  32.5 2.8 %shard_map.79 = (f32[6,256,256]{2,1,0:T(8,128)S(1)}, f32[256,256]{1,0:T(8,128)S(1)}, f32[256,256]{1,0:T(8,128)S(1)}) custom-call(s32[6,4]{1,0:T(8,128)S(1)} %pad_add_fusion.scalars, bf16[2,4,2,256,256]{4,3,2,1,0:T(8,128)(2,1)S(1)} %get-tuple-element.31.left_parts, bf16[2,4,2,256,256]{4,3,2,1,0:T(8,128)(2,1)S(1)} %get-tuple-element.32.right_parts, ...), custom_call_target="tpu_custom_call" | custom-call | flops 1610612736 | bytes 4194304 | tf_op jit(solution)/shard_map/pallas_call | solution.py:149
  35.3 0.1 collective-permute-start.1
  35.4 1.5 %collective-permute-done.1 = f32[256,256]{1,0:T(8,128)S(1)} collective-permute-done((f32[256,256]{1,0:T(8,128)S(1)}, f32[256,256]{1,0:T(8,128)S(1)}, u32[]{:S(2)}, u32[]{:S(2)}) %collective-permute-start.1) | collective-permute-done | bytes 262176 | tf_op jit(solution)/shard_map/ppermute | solution.py:277
  37.0 1.3 collective-permute-start.2
  38.3 3.0 %shard_map.77 = (bf16[2,4,2,256,256]{4,3,2,1,0:T(8,128)(2,1)S(1)}, bf16[2,4,2,256,256]{4,3,2,1,0:T(8,128)(2,1)S(1)}) custom-call(s32[6,4]{1,0:T(8,128)S(1)} %pad_add_fusion.scalars, f32[4,4,256,256]{3,2,1,0:T(8,128)} %left.3, f32[4,4,256,256]{3,2,1,0:T(8,128)} %right.3), custom_call_target="tpu_custom_call" | custom-call | bytes 4194304 | tf_op jit(solution)/shard_map/pallas_call | solution.py:149
  41.2 2.7 %shard_map.80.acc = f32[6,256,256]{2,1,0:T(8,128)S(1)} custom-call(s32[6,4]{1,0:T(8,128)S(1)} %pad_add_fusion.scalars, bf16[2,4,2,256,256]{4,3,2,1,0:T(8,128)(2,1)S(1)} %get-tuple-element.28.left_parts, bf16[2,4,2,256,256]{4,3,2,1,0:T(8,128)(2,1)S(1)} %get-tuple-element.29.right_parts, ...), custom_call_target="tpu_custom_call", output_to_operand_aliasing={{}: (5, {})} | custom-call | flops 1610612736 | bytes 4194304 | tf_op jit(solution)/shard_map/pallas_call | solution.py:149
  43.9 1.8 %collective-permute-done.2.edge = f32[256,256]{1,0:T(8,128)S(1)} collective-permute-done((f32[256,256]{1,0:T(8,128)S(1)}, f32[256,256]{1,0:T(8,128)S(1)}, u32[]{:S(2)}, u32[]{:S(2)}) %collective-permute-start.2) | collective-permute-done | bytes 262176 | tf_op jit(solution)/shard_map/ppermute | solution.py:285
  45.8 0.9 shard_map.81
  46.7 0.0 copy-start
  46.7 0.0 copy-start.1
  46.7 2.4 %collective-permute-start.3 = (f32[8,72,256]{2,1,0:T(8,128)S(1)}, f32[8,72,256]{2,1,0:T(8,128)S(1)}, u32[]{:S(2)}, u32[]{:S(2)}) collective-permute-start(f32[8,72,256]{2,1,0:T(8,128)S(1)} %get-tuple-element.37), channel_id=1, source_target_pairs={{0,16},{16,0},{32,48},{48,32},{64,80},{80,64},{96,112},{112,96},{1... | collective-permute-start | bytes 1769480 | tf_op jit(solution)/shard_map/ppermute | solution.py:277
  49.1 1.6 %collective-permute-done.3 = f32[8,72,256]{2,1,0:T(8,128)S(1)} collective-permute-done((f32[8,72,256]{2,1,0:T(8,128)S(1)}, f32[8,72,256]{2,1,0:T(8,128)S(1)}, u32[]{:S(2)}, u32[]{:S(2)}) %collective-permute-start.3) | collective-permute-done | bytes 589856 | tf_op jit(solution)/shard_map/ppermute | solution.py:277
  50.8 0.1 add.18
  50.9 21.8 %all_to_all.26.parts = f32[8,72,256]{2,1,0:T(8,128)S(1)} all-to-all(f32[8,72,256]{2,1,0:T(8,128)S(1)} %add.18), channel_id=1, replica_groups={{0,32,64,96,128,160,192,224},{16,48,80,112,144,176,208,240},{1,33,65,97..., dimensions={0} | all-to-all | bytes 1179648 | tf_op jit(solution)/shard_map/all_to_all | solution.py:263
  72.6 0.0 copy-done
  72.6 0.0 copy-done.1
  72.6 0.2 shard_map.82
  72.8 11.4 %all_to_all.27.parts = f32[16,8,128]{2,1,0:T(8,128)S(1)} all-to-all(f32[16,8,128]{2,1,0:T(8,128)S(1)} %get-tuple-element.38), channel_id=1, replica_groups=mesh['ops'=16,'sec'=16] {'sec'}, dimensions={0} | all-to-all | bytes 131072 | tf_op jit(solution)/shard_map/all_to_all | solution.py:293
  84.3 0.1 shard_map.83
  84.4 18.2 %all_to_all.28.own = f32[8,72,256]{2,1,0:T(8,128)S(1)} all-to-all(f32[8,72,256]{2,1,0:T(8,128)S(1)} %get-tuple-element.40), channel_id=1, replica_groups={{0,32,64,96,128,160,192,224},{16,48,80,112,144,176,208,240},{1,33,65,97..., dimensions={0} | all-to-all | bytes 1179648 | tf_op jit(solution)/shard_map/all_to_all | solution.py:263
  102.6 4.0 %collective-permute-start.4 = (f32[8,72,256]{2,1,0:T(8,128)S(1)}, f32[8,72,256]{2,1,0:T(8,128)S(1)}, u32[]{:S(2)}, u32[]{:S(2)}) collective-permute-start(f32[8,72,256]{2,1,0:T(8,128)S(1)} %all_to_all.28.own), channel_id=1, source_target_pairs={{0,16},{16,0},{32,48},{48,32},{64,80},{80,64},{96,112},{112,96},{1... | collective-permute-start | bytes 1769480 | tf_op jit(solution)/shard_map/ppermute | solution.py:277
  106.6 1.6 %collective-permute-done.4.other = f32[8,72,256]{2,1,0:T(8,128)S(1)} collective-permute-done((f32[8,72,256]{2,1,0:T(8,128)S(1)}, f32[8,72,256]{2,1,0:T(8,128)S(1)}, u32[]{:S(2)}, u32[]{:S(2)}) %collective-permute-start.4) | collective-permute-done | bytes 589856 | tf_op jit(solution)/shard_map/ppermute | solution.py:277
  108.3 2.8 %shard_map.84 = (f32[6,256,256]{2,1,0:T(8,128)S(1)}, f32[8,16,256]{2,1,0:T(8,128)S(1)}, f32[8,16,256]{2,1,0:T(8,128)S(1)}, f32[2,8,16,256]{3,2,1,0:T(8,128)S(1)}, f32[8,256]{1,0:T(8,128)S(1)}) custom-call(s32[6,4]{1,0:T(8,128)S(1)} %pad_add_fusion.scalars, bf16[2,4,2,256,256]{4,3,2,1,0:T(8,128)(2,1)S(1)} %get-tuple-element.31.left_parts, ...), custom_call_target="tpu_custom_call" | custom-call | flops 1610612736 | bytes 4194304 | tf_op jit(solution)/shard_map/pallas_call | solution.py:149
  111.1 0.6 collective-permute-start.6
  111.7 2.8 %shard_map.85 = (f32[6,256,256]{2,1,0:T(8,128)S(1)}, f32[8,64,256]{2,1,0:T(8,128)S(1)}, f32[8,64,256]{2,1,0:T(8,128)S(1)}) custom-call(s32[6,4]{1,0:T(8,128)S(1)} %pad_add_fusion.scalars, bf16[2,4,2,256,256]{4,3,2,1,0:T(8,128)(2,1)S(1)} %get-tuple-element.28.left_parts, ...), custom_call_target="tpu_custom_call", output_to_operand_aliasing={{0}: (5, {})} | custom-call | flops 1610612736 | bytes 4194304 | tf_op jit(solution)/shard_map/pallas_call | solution.py:149
  114.5 0.2 collective-permute-start.5
  114.7 0.0 collective-permute-done.6
  114.8 1.6 %collective-permute-start.8 = (f32[8,16,256]{2,1,0:T(8,128)S(1)}, f32[8,16,256]{2,1,0:T(8,128)S(1)}, u32[]{:S(2)}, u32[]{:S(2)}) collective-permute-start(f32[8,16,256]{2,1,0:T(8,128)S(1)} %get-tuple-element.52), channel_id=1, source_target_pairs={{0,15},{1,0},{2,1},{3,2},{4,3},{5,4},{6,5},{7,6},{8,7},{9,8},{10,9... | collective-permute-start | bytes 393224 | tf_op jit(solution)/shard_map/ppermute | solution.py:303
  116.3 0.0 collective-permute-start.7
  116.3 3.2 %collective-permute-done.8.from_high = f32[8,16,256]{2,1,0:T(8,128)S(1)} collective-permute-done((f32[8,16,256]{2,1,0:T(8,128)S(1)}, f32[8,16,256]{2,1,0:T(8,128)S(1)}, u32[]{:S(2)}, u32[]{:S(2)}) %collective-permute-start.8) | collective-permute-done | bytes 131104 | tf_op jit(solution)/shard_map/ppermute | solution.py:303
  119.6 4.5 %collective-permute-done.7.from_low = f32[8,16,256]{2,1,0:T(8,128)S(1)} collective-permute-done((f32[8,16,256]{2,1,0:T(8,128)S(1)}, f32[8,16,256]{2,1,0:T(8,128)S(1)}, u32[]{:S(2)}, u32[]{:S(2)}) %collective-permute-start.7) | collective-permute-done | bytes 131104 | tf_op jit(solution)/shard_map/ppermute | solution.py:304
  124.0 0.0 collective-permute-done.5.theirs
  124.0 0.7 shard_map.86
  124.7 17.7 %all_to_all.29.parts = f32[8,64,256]{2,1,0:T(8,128)S(1)} all-to-all(f32[8,64,256]{2,1,0:T(8,128)S(1)} %shard_map.86), channel_id=1, replica_groups={{0,32,64,96,128,160,192,224},{16,48,80,112,144,176,208,240},{1,33,65,97..., dimensions={0} | all-to-all | bytes 1048576 | tf_op jit(solution)/shard_map/all_to_all | solution.py:263
  142.4 0.8 shard_map.87
  (3 shorter events, 0.1 us)
Async XLA Ops:
  27.1 5.4 %collective-permute-start = (f32[8,64,256]{2,1,0:T(8,128)S(1)}, f32[8,64,256]{2,1,0:T(8,128)S(1)}, u32[]{:S(2)}, u32[]{:S(2)}) collective-permute-start(f32[8,64,256]{2,1,0:T(8,128)S(1)} %all_to_all.25.own), channel_id=1, source_target_pairs={{0,16},{16,0},{32,48},{48,32},{64,80},{80,64},{96,112},{112,96},{1... | collective-permute-start | bytes 1572872 | tf_op jit(solution)/shard_map/ppermute | solution.py:277
  35.3 1.6 %collective-permute-start.1 = (f32[256,256]{1,0:T(8,128)S(1)}, f32[256,256]{1,0:T(8,128)S(1)}, u32[]{:S(2)}, u32[]{:S(2)}) collective-permute-start(f32[256,256]{1,0:T(8,128)S(1)} %get-tuple-element.35), channel_id=1, source_target_pairs={{0,16},{16,0},{32,48},{48,32},{64,80},{80,64},{96,112},{112,96},{1... | collective-permute-start | bytes 786440 | tf_op jit(solution)/shard_map/ppermute | solution.py:277
  37.0 8.8 %collective-permute-start.2 = (f32[256,256]{1,0:T(8,128)S(1)}, f32[256,256]{1,0:T(8,128)S(1)}, u32[]{:S(2)}, u32[]{:S(2)}) collective-permute-start(f32[256,256]{1,0:T(8,128)S(1)} %add.17), channel_id=1, source_target_pairs={{0,15},{1,0},{2,1},{3,2},{4,3},{5,4},{6,5},{7,6},{8,7},{9,8},{10,9... | collective-permute-start | bytes 786440 | tf_op jit(solution)/shard_map/ppermute | solution.py:285
  46.7 25.9 %copy-start = (f32[4,16,256]{2,1,0:T(8,128)S(1)}, f32[4,16,256]{2,1,0:T(8,128)}, u32[]{:S(2)}) copy-start(f32[4,16,256]{2,1,0:T(8,128)} %param.6) | copy-start | bytes 196612
  46.7 25.9 %copy-start.1 = (f32[4,16,256]{2,1,0:T(8,128)S(1)}, f32[4,16,256]{2,1,0:T(8,128)}, u32[]{:S(2)}) copy-start(f32[4,16,256]{2,1,0:T(8,128)} %param.9) | copy-start | bytes 196612
  46.7 4.0 %collective-permute-start.3 = (f32[8,72,256]{2,1,0:T(8,128)S(1)}, f32[8,72,256]{2,1,0:T(8,128)S(1)}, u32[]{:S(2)}, u32[]{:S(2)}) collective-permute-start(f32[8,72,256]{2,1,0:T(8,128)S(1)} %get-tuple-element.37), channel_id=1, source_target_pairs={{0,16},{16,0},{32,48},{48,32},{64,80},{80,64},{96,112},{112,96},{1... | collective-permute-start | bytes 1769480 | tf_op jit(solution)/shard_map/ppermute | solution.py:277
  102.6 5.6 %collective-permute-start.4 = (f32[8,72,256]{2,1,0:T(8,128)S(1)}, f32[8,72,256]{2,1,0:T(8,128)S(1)}, u32[]{:S(2)}, u32[]{:S(2)}) collective-permute-start(f32[8,72,256]{2,1,0:T(8,128)S(1)} %all_to_all.28.own), channel_id=1, source_target_pairs={{0,16},{16,0},{32,48},{48,32},{64,80},{80,64},{96,112},{112,96},{1... | collective-permute-start | bytes 1769480 | tf_op jit(solution)/shard_map/ppermute | solution.py:277
  111.1 3.6 %collective-permute-start.6 = (f32[2,8,16,256]{3,2,1,0:T(8,128)S(1)}, f32[2,8,16,256]{3,2,1,0:T(8,128)S(1)}, u32[]{:S(2)}, u32[]{:S(2)}) collective-permute-start(f32[2,8,16,256]{3,2,1,0:T(8,128)S(1)} %get-tuple-element.45), channel_id=1, source_target_pairs={{0,16},{16,0},{32,48},{48,32},{64,80},{80,64},{96,112},{112,96},{1... | collective-permute-start | bytes 786440 | tf_op jit(solution)/shard_map/ppermute | solution.py:277
  114.5 9.5 %collective-permute-start.5 = (f32[8,64,256]{2,1,0:T(8,128)S(1)}, f32[8,64,256]{2,1,0:T(8,128)S(1)}, u32[]{:S(2)}, u32[]{:S(2)}) collective-permute-start(f32[8,64,256]{2,1,0:T(8,128)S(1)} %get-tuple-element.43), channel_id=1, source_target_pairs={{0,16},{16,0},{32,48},{48,32},{64,80},{80,64},{96,112},{112,96},{1... | collective-permute-start | bytes 1572872 | tf_op jit(solution)/shard_map/ppermute | solution.py:277
  114.8 4.8 %collective-permute-start.8 = (f32[8,16,256]{2,1,0:T(8,128)S(1)}, f32[8,16,256]{2,1,0:T(8,128)S(1)}, u32[]{:S(2)}, u32[]{:S(2)}) collective-permute-start(f32[8,16,256]{2,1,0:T(8,128)S(1)} %get-tuple-element.52), channel_id=1, source_target_pairs={{0,15},{1,0},{2,1},{3,2},{4,3},{5,4},{6,5},{7,6},{8,7},{9,8},{10,9... | collective-permute-start | bytes 393224 | tf_op jit(solution)/shard_map/ppermute | solution.py:303
  116.3 7.7 %collective-permute-start.7 = (f32[8,16,256]{2,1,0:T(8,128)S(1)}, f32[8,16,256]{2,1,0:T(8,128)S(1)}, u32[]{:S(2)}, u32[]{:S(2)}) collective-permute-start(f32[8,16,256]{2,1,0:T(8,128)S(1)} %get-tuple-element.53), channel_id=1, source_target_pairs={{0,1},{1,2},{2,3},{3,4},{4,5},{5,6},{6,7},{7,8},{8,9},{9,10},{10,1... | collective-permute-start | bytes 393224 | tf_op jit(solution)/shard_map/ppermute | solution.py:304

commit v5 on v4

--- a/solution.py
+++ b/solution.py
@@ -11,6 +11,7 @@
 F32 = jnp.float32
 BF16 = jnp.bfloat16
 BLK = 256
+HALF = 128
 ROWS = 16
 NZ = 8
 NT = (((1,), (1,)), ((), ()))
@@ -33,12 +34,23 @@
     return lax.dot_general(a, b, dims, preferred_element_type=F32)
 
 
+def rows_at(x, z, pair):
+    rows = slice(pair * ROWS, (pair + 1) * ROWS)
+    if x.shape[2] == BLK:
+        return x[z, rows, :]
+    return jnp.concatenate([x[z, rows, :], x[z, 64 + pair * ROWS : 64 + (pair + 1) * ROWS, :]], axis=1)
+
+
+def put_rows(x, z, rows, value):
+    x[z, rows, :] = value[:, :HALF]
+    x[z, 64 + rows.start : 64 + rows.stop, :] = value[:, HALF:]
+
+
 def items(pairs, scalars, parts, own, other, acc):
     for slot, pair in enumerate(pairs):
-        rows = slice(pair * ROWS, (pair + 1) * ROWS)
         pieces = []
         for z in range(NZ):
-            a, b = own[z, rows, :], other[z, rows, :]
+            a, b = rows_at(own, z, pair), rows_at(other, z, pair)
             pieces += [jnp.where(scalars[5, 0] == 0, a, b), jnp.where(scalars[5, 0] == 0, b, a)]
         vh, vl = split(jnp.concatenate(pieces, axis=0))
         for term in range(4):
@@ -77,16 +89,36 @@
     return parts
 
 
-def parts_kernel(pairs, scalars, left, right, *rest):
-    *_, left_parts, right_parts, blocks, semaphores = rest
-    copies = copies_of(pairs, left, right, blocks, semaphores)
-    for copy in copies:
-        copy.start()
+def split_parts(pairs, scalars, copies, blocks, left_parts, right_parts):
     parts = fresh_parts(scalars, blocks, left_parts, right_parts)
     for i, (slot, term) in enumerate((slot, term) for slot in range(2) for term in range(4)):
         copies[2 * i].wait()
         copies[2 * i + 1].wait()
         parts(slot, pairs[slot], term)
+
+
+def first_parts_kernel(left, right, coupling, charges, left_parts, right_parts, scalars, blocks, semaphores, ends):
+    small = [
+        pltpu.make_async_copy(coupling, scalars.at[pl.ds(0, 4), :], ends.at[0]),
+        pltpu.make_async_copy(charges, scalars.at[4], ends.at[1]),
+    ]
+    copies = copies_of(EDGES, left, right, blocks, semaphores)
+    for copy in small + copies:
+        copy.start()
+    for copy in small:
+        copy.wait()
+    scalars[5, 0] = lax.rem(lax.axis_index("ops"), 2)
+    scalars[5, 1] = lax.axis_index("sec")
+    scalars[5, 2] = 0
+    scalars[5, 3] = 0
+    split_parts(EDGES, scalars, copies, blocks, left_parts, right_parts)
+
+
+def parts_kernel(scalars, left, right, left_parts, right_parts, blocks, semaphores):
+    copies = copies_of(INNER, left, right, blocks, semaphores)
+    for copy in copies:
+        copy.start()
+    split_parts(INNER, scalars, copies, blocks, left_parts, right_parts)
 
 
 def edges_of(acc, scalars, kept, given):
@@ -113,7 +145,7 @@
         high[z] = acc[5, rows_of(z, core), :]
         given[0, z] = acc[0, rows_of(z, 1 - core), :]
         given[1, z] = acc[5, rows_of(z, 1 - core), :]
-    totals[...] = added(own[:, 64:72, :]) + added(other[:, 64:72, :])
+    totals[...] = added(own[:, 128:136, :]) + added(other[:, 128:136, :])
 
 
 def inner_kernel(scalars, left_parts, right_parts, own, other, start, acc):
@@ -177,18 +209,18 @@
             place = slice(pair * ROWS, (pair + 1) * ROWS)
             a = jnp.where(scalars[5, 0] == 0, pieces[0], pieces[1])
             b = jnp.where(scalars[5, 0] == 0, pieces[1], pieces[0])
-            mine[z, place, :] = a
-            theirs[z, place, :] = b
+            put_rows(mine, z, place, a)
+            put_rows(theirs, z, place, b)
             va, vb = own[z, place, :], other[z, place, :]
             d = a * va + b * vb
             n = va * va + vb * vb
             dots += d[:8] + d[8:]
             norms += n[:8] + n[8:]
-    row = lax.broadcasted_iota(jnp.int32, (8, BLK), 0)
+    row = lax.broadcasted_iota(jnp.int32, (8, HALF), 0)
     sums = jnp.where(row == 0, jnp.sum(dots), 0.0) + jnp.where(row == 1, jnp.sum(norms) * (1.0 / 16), 0.0)
     for z in range(NZ):
-        mine[z, 64:72, :] = sums
-        theirs[z, 64:72, :] = sums
+        mine[z, 128:136, :] = sums
+        theirs[z, 128:136, :] = sums
 
 
 def added(parts):
@@ -200,11 +232,12 @@
 
 def image_kernel(parts, vector, weights, image, sums):
     total = added(parts)
-    correlation, norm = total[64:65, 0:1], total[65:66, 0:1]
+    correlation, norm = total[128:129, 0:1], total[129:130, 0:1]
+    summed = jnp.concatenate([total[:64], total[64:128]], axis=1)
     usable = norm > 1e-18
     near = jnp.where(usable, correlation, 0.0) / jnp.where(usable, norm, 1.0)
-    image[...] = total[:64]
-    rest = (total[:64] - near * vector[...]) / weights[...]
+    image[...] = summed
+    rest = (summed - near * vector[...]) / weights[...]
     weighted = vector[...] / weights[...]
     products = (vector[...] * rest, vector[...] * weighted, rest * rest, rest * weighted, weighted * weighted)
     values = [correlation, norm, *(jnp.sum(x, keepdims=True) for x in products), near]
@@ -230,11 +263,11 @@
     norm[...] = jnp.broadcast_to(total[:, 0:1], (8, BLK))
     value = (image[...] - rayleigh[:, 0:1] * vector[...]) / weights[...]
     scaled[...] = value
-    row = lax.broadcasted_iota(jnp.int32, (8, BLK), 0)
+    row = lax.broadcasted_iota(jnp.int32, (8, HALF), 0)
     rows = jnp.where(row == 0, along[:, 0:1], squares[:, 0:1])
     for z in range(NZ):
-        sent[z, :64, :] = value
-        sent[z, 64:72, :] = rows
+        put_rows(sent, z, slice(0, 64), value)
+        sent[z, 128:136, :] = rows
 
 
 def finish_kernel(entries, parts, image, vector, scaled, norm, totals, correction, image_new):
@@ -265,12 +298,8 @@
 
 def on_device(wavefunction, left_operators, right_operators, preconditioner, charges, coupling):
     entries = wavefunction.size * lax.axis_size("ops") * lax.axis_size("sec")
-    core, position = lax.axis_index("ops") % 2, lax.axis_index("sec")
-    place = jnp.where(jnp.arange(4) == 0, core, position).astype(jnp.int32)
-    scalars = jnp.concatenate([coupling, charges[None], place[None]])
     slab = wavefunction.reshape(64, BLK)
     weights = preconditioner.reshape(64, BLK)
-    slab, scalars = lax.optimization_barrier((slab, scalars))
     operators = [pltpu.with_memory_space_constraint(x, pltpu.HBM) for x in (left_operators, right_operators)]
 
     def swap(x):
@@ -279,25 +308,33 @@
     own = exchange(jnp.broadcast_to(slab[None], (NZ, 64, BLK)))
     other = swap(own)
     scratch = [pltpu.VMEM(BLOCKS, F32), COPIES]
-    split_edges, split_inner = (functools.partial(parts_kernel, pairs) for pairs in (EDGES, INNER))
-    edge_parts = on_blocks(split_edges, [PARTS] * 2, scalars, operators, [], scratch, flops=0)
+    hbm = pl.BlockSpec(memory_space=pltpu.HBM)
+    *edge_parts, scalars = pl.pallas_call(
+        first_parts_kernel,
+        in_specs=[hbm] * 4,
+        out_specs=[VMEM, VMEM, SMEM],
+        out_shape=[PARTS, PARTS, shape(6, 4, dtype=jnp.int32)],
+        scratch_shapes=[*scratch, pltpu.SemaphoreType.DMA((2,))],
+        compiler_params=PARAMS,
+        cost_estimate=pl.CostEstimate(flops=0, bytes_accessed=8 * 2**19, transcendentals=0),
+    )(*operators, *(pltpu.with_memory_space_constraint(x, pltpu.HBM) for x in (coupling, charges)))
     acc, kept, given = on_blocks(edge_kernel, [ACC, BLOCK, BLOCK], scalars, [], [*edge_parts, own, other])
     edge = lax.ppermute(kept + swap(given), ("ops", "sec"), TO_EDGES)
-    inner_parts = on_blocks(split_inner, [PARTS] * 2, scalars, operators, [], scratch, flops=0)
+    inner_parts = on_blocks(parts_kernel, [PARTS] * 2, scalars, operators, [], scratch, flops=0)
     (acc,) = on_blocks(inner_kernel, [ACC], scalars, [], [*inner_parts, own, other, acc], alias={5: 0})
-    halves, vectors = [shape(NZ, 72, BLK)] * 2, [acc, edge, own, other]
+    halves, vectors = [shape(NZ, 136, HALF)] * 2, [acc, edge, own, other]
     mine, theirs = on_blocks(arrange_kernel, halves, scalars, [], vectors, flops=0)
     parts = exchange(mine + swap(theirs))
 
     image, sums = local(image_kernel, [shape(64, BLK), shape(16, 8, 128)], parts, slab, weights)
     sums = lax.all_to_all(sums, "sec", 0, 0)
-    outs = [shape(64, BLK), shape(8, BLK), shape(NZ, 72, BLK)]
+    outs = [shape(64, BLK), shape(8, BLK), shape(NZ, 136, HALF)]
     scaled, norm, sent = local(scaled_kernel, outs, sums, image, slab, weights)
 
     own = exchange(sent)
     other = swap(own)
     strip = shape(NZ, ROWS, BLK)
-    outs = [ACC, strip, strip, shape(2, NZ, ROWS, BLK), shape(8, BLK)]
+    outs = [ACC, strip, strip, shape(2, NZ, ROWS, BLK), shape(8, HALF)]
     acc, low, high, given, totals = on_blocks(last_edge_kernel, outs, scalars, [], [*edge_parts, own, other])
     given = swap(given)
     from_high = lax.ppermute(low + given[0], "sec", DOWN)

time: 144 us -> 141 us (0.979)
  blocking collectives: 93.9 us -> 92.2 us
    pallas_call x8 -> x7, Pallas kernels: 18.6 us -> 15.7 us  [on_blocks(): pl.pallas_call(kernel, in_specs=[SMEM] + [pl.BlockSpec(memory_space=pltpu...]
    pallas_call x0 -> x1, Pallas kernels: none -> 2.94 us  [on_device(): pl.pallas_call(first_parts_kernel, in_specs=[hbm] * 4, out_specs=[VMEM, V...]
    all_to_all x4, blocking collectives: 82.5 us -> 80.8 us  [exchange(): return lax.all_to_all(parts, 'ops', 0, 0, axis_index_groups=SAME_CORE)]
where the time goes in v5:
time: 141 us; the launch traced here: 140 us
  blocking collectives  92.2 us (65%)
  Pallas kernels  19.7 us (14%)
  waiting for transfers between devices  14.2 us (10%)
  starting transfers between devices  12.6 us (9%)
    all_to_all x4, blocking collectives, exchange(): return lax.all_to_all(parts, 'ops', 0, 0, axis_index_groups=SAME_CORE)  80.8 us
    pallas_call x7, Pallas kernels, on_blocks(): pl.pallas_call(kernel, in_specs=[SMEM] + [pl.BlockSpec(memory_space=pltpu...  15.7 us
    all_to_all x1, blocking collectives, on_device(): sums = lax.all_to_all(sums, 'sec', 0, 0)  11.4 us
    ppermute x6, starting transfers between devices, swap(): return lax.ppermute(x, 'ops', SWAP)  9.75 us
    ppermute x6, waiting for transfers between devices, swap(): return lax.ppermute(x, 'ops', SWAP)  4.7 us
    ppermute x1, waiting for transfers between devices, on_device(): from_low = lax.ppermute(high + given[1], 'sec', UP)  4.5 us
    ppermute x1, waiting for transfers between devices, on_device(): from_high = lax.ppermute(low + given[0], 'sec', DOWN)  3.21 us
    pallas_call x1, Pallas kernels, on_device(): pl.pallas_call(first_parts_kernel, in_specs=[hbm] * 4, out_specs=[VMEM, V...  2.94 us
  transfers between devices with their start and end apart: 9, of which 6 were waited for; matrix products, arithmetic and copies ran while one was open for 0% of the time, Pallas kernels for 8%

profile of v5, /device:TPU:1, one launch (start us, length us, event | category | flops | bytes accessed | tf_op | source)
XLA Modules:
  0.0 140.5 jit_solution(14283052256923022680)
XLA Ops:
  0.6 0.9 broadcast_in_dim.8
  1.5 24.8 %all_to_all.25.own = f32[8,64,256]{2,1,0:T(8,128)S(1)} all-to-all(f32[8,64,256]{2,1,0:T(8,128)S(1)} %broadcast_in_dim.8), channel_id=1, replica_groups={{0,32,64,96,128,160,192,224},{16,48,80,112,144,176,208,240},{1,33,65,97..., dimensions={0} | all-to-all | bytes 1048576 | tf_op jit(solution)/shard_map/all_to_all | solution.py:296
  26.3 2.5 %collective-permute-start = (f32[8,64,256]{2,1,0:T(8,128)S(1)}, f32[8,64,256]{2,1,0:T(8,128)S(1)}, u32[]{:S(2)}, u32[]{:S(2)}) collective-permute-start(f32[8,64,256]{2,1,0:T(8,128)S(1)} %all_to_all.25.own), channel_id=1, source_target_pairs={{0,16},{16,0},{32,48},{48,32},{64,80},{80,64},{96,112},{112,96},{1... | collective-permute-start | bytes 1572872 | tf_op jit(solution)/shard_map/ppermute | solution.py:306
  28.8 2.9 %shard_map.77 = (bf16[2,4,2,256,256]{4,3,2,1,0:T(8,128)(2,1)S(1)}, bf16[2,4,2,256,256]{4,3,2,1,0:T(8,128)(2,1)S(1)}, s32[6,4]{1,0:T(8,128)S(1)}) custom-call(f32[4,4,256,256]{3,2,1,0:T(8,128)} %left.3, f32[4,4,256,256]{3,2,1,0:T(8,128)} %right.3, s32[4,4]{1,0:T(4,128)} %coupling.1, s32[4]{0:T(128)} %charges.1), custom_call_target="tpu_custom_call" | custom-call | bytes 4194304 | tf_op jit(solution)/shard_map/pallas_call | solution.py:312
  31.7 0.0 collective-permute-done.other
  31.7 2.8 %shard_map.79 = (f32[6,256,256]{2,1,0:T(8,128)S(1)}, f32[256,256]{1,0:T(8,128)S(1)}, f32[256,256]{1,0:T(8,128)S(1)}) custom-call(s32[6,4]{1,0:T(8,128)S(1)} %get-tuple-element.26.scalars, bf16[2,4,2,256,256]{4,3,2,1,0:T(8,128)(2,1)S(1)} %get-tuple-element.29.left_parts, bf16[2,4,2,256,256]{4,3,2,1,0:T(8,128)(2,1)S(1)} %get-tuple-element.30.right_parts, ...), custom_call_target="tpu_custom_call" | custom-call | flops 1610612736 | bytes 4194304 | tf_op jit(solution)/shard_map/pallas_call | solution.py:181
  34.6 0.1 collective-permute-start.1
  34.7 1.5 %collective-permute-done.1 = f32[256,256]{1,0:T(8,128)S(1)} collective-permute-done((f32[256,256]{1,0:T(8,128)S(1)}, f32[256,256]{1,0:T(8,128)S(1)}, u32[]{:S(2)}, u32[]{:S(2)}) %collective-permute-start.1) | collective-permute-done | bytes 262176 | tf_op jit(solution)/shard_map/ppermute | solution.py:306
  36.2 1.3 collective-permute-start.2
  37.5 3.0 %shard_map.78 = (bf16[2,4,2,256,256]{4,3,2,1,0:T(8,128)(2,1)S(1)}, bf16[2,4,2,256,256]{4,3,2,1,0:T(8,128)(2,1)S(1)}) custom-call(s32[6,4]{1,0:T(8,128)S(1)} %get-tuple-element.26.scalars, f32[4,4,256,256]{3,2,1,0:T(8,128)} %left.3, f32[4,4,256,256]{3,2,1,0:T(8,128)} %right.3), custom_call_target="tpu_custom_call" | custom-call | bytes 4194304 | tf_op jit(solution)/shard_map/pallas_call | solution.py:181
  40.5 2.7 %shard_map.80.acc = f32[6,256,256]{2,1,0:T(8,128)S(1)} custom-call(s32[6,4]{1,0:T(8,128)S(1)} %get-tuple-element.26.scalars, bf16[2,4,2,256,256]{4,3,2,1,0:T(8,128)(2,1)S(1)} %get-tuple-element.27.left_parts, bf16[2,4,2,256,256]{4,3,2,1,0:T(8,128)(2,1)S(1)} %get-tuple-element.28.right_parts, ...), custom_call_target="tpu_custom_call", output_to_operand_aliasing={{}: (5, {})} | custom-call | flops 1610612736 | bytes 4194304 | tf_op jit(solution)/shard_map/pallas_call | solution.py:181
  43.2 1.8 %collective-permute-done.2.edge = f32[256,256]{1,0:T(8,128)S(1)} collective-permute-done((f32[256,256]{1,0:T(8,128)S(1)}, f32[256,256]{1,0:T(8,128)S(1)}, u32[]{:S(2)}, u32[]{:S(2)}) %collective-permute-start.2) | collective-permute-done | bytes 262176 | tf_op jit(solution)/shard_map/ppermute | solution.py:322
  45.0 0.9 shard_map.81
  45.9 0.0 copy-start
  46.0 0.0 copy-start.1
  46.0 2.4 %collective-permute-start.3 = (f32[8,136,128]{2,1,0:T(8,128)S(1)}, f32[8,136,128]{2,1,0:T(8,128)S(1)}, u32[]{:S(2)}, u32[]{:S(2)}) collective-permute-start(f32[8,136,128]{2,1,0:T(8,128)S(1)} %get-tuple-element.35), channel_id=1, source_target_pairs={{0,16},{16,0},{32,48},{48,32},{64,80},{80,64},{96,112},{112,96},{1... | collective-permute-start | bytes 1671176 | tf_op jit(solution)/shard_map/ppermute | solution.py:306
  48.4 1.6 %collective-permute-done.3 = f32[8,136,128]{2,1,0:T(8,128)S(1)} collective-permute-done((f32[8,136,128]{2,1,0:T(8,128)S(1)}, f32[8,136,128]{2,1,0:T(8,128)S(1)}, u32[]{:S(2)}, u32[]{:S(2)}) %collective-permute-start.3) | collective-permute-done | bytes 557088 | tf_op jit(solution)/shard_map/ppermute | solution.py:306
  50.0 0.1 add.13
  50.0 20.7 %all_to_all.26.parts = f32[8,136,128]{2,1,0:T(8,128)S(1)} all-to-all(f32[8,136,128]{2,1,0:T(8,128)S(1)} %add.13), channel_id=1, replica_groups={{0,32,64,96,128,160,192,224},{16,48,80,112,144,176,208,240},{1,33,65,97..., dimensions={0} | all-to-all | bytes 1114112 | tf_op jit(solution)/shard_map/all_to_all | solution.py:296
  70.7 0.0 copy-done
  70.7 0.0 copy-done.1
  70.7 0.2 shard_map.82
  70.9 11.4 %all_to_all.27.parts = f32[16,8,128]{2,1,0:T(8,128)S(1)} all-to-all(f32[16,8,128]{2,1,0:T(8,128)S(1)} %get-tuple-element.36), channel_id=1, replica_groups=mesh['ops'=16,'sec'=16] {'sec'}, dimensions={0} | all-to-all | bytes 131072 | tf_op jit(solution)/shard_map/all_to_all | solution.py:330
  82.4 0.1 shard_map.83
  82.5 17.6 %all_to_all.28.own = f32[8,136,128]{2,1,0:T(8,128)S(1)} all-to-all(f32[8,136,128]{2,1,0:T(8,128)S(1)} %get-tuple-element.38), channel_id=1, replica_groups={{0,32,64,96,128,160,192,224},{16,48,80,112,144,176,208,240},{1,33,65,97..., dimensions={0} | all-to-all | bytes 1114112 | tf_op jit(solution)/shard_map/all_to_all | solution.py:296
  100.1 3.9 %collective-permute-start.4 = (f32[8,136,128]{2,1,0:T(8,128)S(1)}, f32[8,136,128]{2,1,0:T(8,128)S(1)}, u32[]{:S(2)}, u32[]{:S(2)}) collective-permute-start(f32[8,136,128]{2,1,0:T(8,128)S(1)} %all_to_all.28.own), channel_id=1, source_target_pairs={{0,16},{16,0},{32,48},{48,32},{64,80},{80,64},{96,112},{112,96},{1... | collective-permute-start | bytes 1671176 | tf_op jit(solution)/shard_map/ppermute | solution.py:306
  104.0 1.6 %collective-permute-done.4.other = f32[8,136,128]{2,1,0:T(8,128)S(1)} collective-permute-done((f32[8,136,128]{2,1,0:T(8,128)S(1)}, f32[8,136,128]{2,1,0:T(8,128)S(1)}, u32[]{:S(2)}, u32[]{:S(2)}) %collective-permute-start.4) | collective-permute-done | bytes 557088 | tf_op jit(solution)/shard_map/ppermute | solution.py:306
  105.6 2.8 %shard_map.84 = (f32[6,256,256]{2,1,0:T(8,128)S(1)}, f32[8,16,256]{2,1,0:T(8,128)S(1)}, f32[8,16,256]{2,1,0:T(8,128)S(1)}, f32[2,8,16,256]{3,2,1,0:T(8,128)S(1)}, f32[8,128]{1,0:T(8,128)S(1)}) custom-call(s32[6,4]{1,0:T(8,128)S(1)} %get-tuple-element.26.scalars, bf16[2,4,2,256,256]{4,3,2,1,0:T(8,128)(2,1)S(1)} %get-tuple-element.29.left_parts, ...), custom_call_target="tpu_custom_call" | custom-call | flops 1610612736 | bytes 4194304 | tf_op jit(solution)/shard_map/pallas_call | solution.py:181
  108.4 0.6 collective-permute-start.6
  109.1 2.8 %shard_map.85 = (f32[6,256,256]{2,1,0:T(8,128)S(1)}, f32[8,64,256]{2,1,0:T(8,128)S(1)}, f32[8,64,256]{2,1,0:T(8,128)S(1)}) custom-call(s32[6,4]{1,0:T(8,128)S(1)} %get-tuple-element.26.scalars, bf16[2,4,2,256,256]{4,3,2,1,0:T(8,128)(2,1)S(1)} %get-tuple-element.27.left_parts, ...), custom_call_target="tpu_custom_call", output_to_operand_aliasing={{0}: (5, {})} | custom-call | flops 1610612736 | bytes 4194304 | tf_op jit(solution)/shard_map/pallas_call | solution.py:181
  111.8 0.2 collective-permute-start.5
  112.0 0.0 collective-permute-done.6
  112.1 1.6 %collective-permute-start.8 = (f32[8,16,256]{2,1,0:T(8,128)S(1)}, f32[8,16,256]{2,1,0:T(8,128)S(1)}, u32[]{:S(2)}, u32[]{:S(2)}) collective-permute-start(f32[8,16,256]{2,1,0:T(8,128)S(1)} %get-tuple-element.50), channel_id=1, source_target_pairs={{0,15},{1,0},{2,1},{3,2},{4,3},{5,4},{6,5},{7,6},{8,7},{9,8},{10,9... | collective-permute-start | bytes 393224 | tf_op jit(solution)/shard_map/ppermute | solution.py:340
  113.7 0.0 collective-permute-start.7
  113.7 3.2 %collective-permute-done.8.from_high = f32[8,16,256]{2,1,0:T(8,128)S(1)} collective-permute-done((f32[8,16,256]{2,1,0:T(8,128)S(1)}, f32[8,16,256]{2,1,0:T(8,128)S(1)}, u32[]{:S(2)}, u32[]{:S(2)}) %collective-permute-start.8) | collective-permute-done | bytes 131104 | tf_op jit(solution)/shard_map/ppermute | solution.py:340
  116.9 4.5 %collective-permute-done.7.from_low = f32[8,16,256]{2,1,0:T(8,128)S(1)} collective-permute-done((f32[8,16,256]{2,1,0:T(8,128)S(1)}, f32[8,16,256]{2,1,0:T(8,128)S(1)}, u32[]{:S(2)}, u32[]{:S(2)}) %collective-permute-start.7) | collective-permute-done | bytes 131104 | tf_op jit(solution)/shard_map/ppermute | solution.py:341
  121.4 0.0 collective-permute-done.5.theirs
  121.4 0.7 shard_map.86
  122.1 17.7 %all_to_all.29.parts = f32[8,64,256]{2,1,0:T(8,128)S(1)} all-to-all(f32[8,64,256]{2,1,0:T(8,128)S(1)} %shard_map.86), channel_id=1, replica_groups={{0,32,64,96,128,160,192,224},{16,48,80,112,144,176,208,240},{1,33,65,97..., dimensions={0} | all-to-all | bytes 1048576 | tf_op jit(solution)/shard_map/all_to_all | solution.py:296
  139.8 0.7 shard_map.87
  (2 shorter events, 0.1 us)
Async XLA Ops:
  26.3 5.4 %collective-permute-start = (f32[8,64,256]{2,1,0:T(8,128)S(1)}, f32[8,64,256]{2,1,0:T(8,128)S(1)}, u32[]{:S(2)}, u32[]{:S(2)}) collective-permute-start(f32[8,64,256]{2,1,0:T(8,128)S(1)} %all_to_all.25.own), channel_id=1, source_target_pairs={{0,16},{16,0},{32,48},{48,32},{64,80},{80,64},{96,112},{112,96},{1... | collective-permute-start | bytes 1572872 | tf_op jit(solution)/shard_map/ppermute | solution.py:306
  34.6 1.6 %collective-permute-start.1 = (f32[256,256]{1,0:T(8,128)S(1)}, f32[256,256]{1,0:T(8,128)S(1)}, u32[]{:S(2)}, u32[]{:S(2)}) collective-permute-start(f32[256,256]{1,0:T(8,128)S(1)} %get-tuple-element.33), channel_id=1, source_target_pairs={{0,16},{16,0},{32,48},{48,32},{64,80},{80,64},{96,112},{112,96},{1... | collective-permute-start | bytes 786440 | tf_op jit(solution)/shard_map/ppermute | solution.py:306
  36.2 8.8 %collective-permute-start.2 = (f32[256,256]{1,0:T(8,128)S(1)}, f32[256,256]{1,0:T(8,128)S(1)}, u32[]{:S(2)}, u32[]{:S(2)}) collective-permute-start(f32[256,256]{1,0:T(8,128)S(1)} %add.12), channel_id=1, source_target_pairs={{0,15},{1,0},{2,1},{3,2},{4,3},{5,4},{6,5},{7,6},{8,7},{9,8},{10,9... | collective-permute-start | bytes 786440 | tf_op jit(solution)/shard_map/ppermute | solution.py:322
  45.9 24.8 %copy-start = (f32[4,16,256]{2,1,0:T(8,128)S(1)}, f32[4,16,256]{2,1,0:T(8,128)}, u32[]{:S(2)}) copy-start(f32[4,16,256]{2,1,0:T(8,128)} %param.6) | copy-start | bytes 196612
  46.0 24.7 %copy-start.1 = (f32[4,16,256]{2,1,0:T(8,128)S(1)}, f32[4,16,256]{2,1,0:T(8,128)}, u32[]{:S(2)}) copy-start(f32[4,16,256]{2,1,0:T(8,128)} %param.9) | copy-start | bytes 196612
  46.0 4.0 %collective-permute-start.3 = (f32[8,136,128]{2,1,0:T(8,128)S(1)}, f32[8,136,128]{2,1,0:T(8,128)S(1)}, u32[]{:S(2)}, u32[]{:S(2)}) collective-permute-start(f32[8,136,128]{2,1,0:T(8,128)S(1)} %get-tuple-element.35), channel_id=1, source_target_pairs={{0,16},{16,0},{32,48},{48,32},{64,80},{80,64},{96,112},{112,96},{1... | collective-permute-start | bytes 1671176 | tf_op jit(solution)/shard_map/ppermute | solution.py:306
  100.1 5.5 %collective-permute-start.4 = (f32[8,136,128]{2,1,0:T(8,128)S(1)}, f32[8,136,128]{2,1,0:T(8,128)S(1)}, u32[]{:S(2)}, u32[]{:S(2)}) collective-permute-start(f32[8,136,128]{2,1,0:T(8,128)S(1)} %all_to_all.28.own), channel_id=1, source_target_pairs={{0,16},{16,0},{32,48},{48,32},{64,80},{80,64},{96,112},{112,96},{1... | collective-permute-start | bytes 1671176 | tf_op jit(solution)/shard_map/ppermute | solution.py:306
  108.4 3.6 %collective-permute-start.6 = (f32[2,8,16,256]{3,2,1,0:T(8,128)S(1)}, f32[2,8,16,256]{3,2,1,0:T(8,128)S(1)}, u32[]{:S(2)}, u32[]{:S(2)}) collective-permute-start(f32[2,8,16,256]{3,2,1,0:T(8,128)S(1)} %get-tuple-element.43), channel_id=1, source_target_pairs={{0,16},{16,0},{32,48},{48,32},{64,80},{80,64},{96,112},{112,96},{1... | collective-permute-start | bytes 786440 | tf_op jit(solution)/shard_map/ppermute | solution.py:306
  111.8 9.6 %collective-permute-start.5 = (f32[8,64,256]{2,1,0:T(8,128)S(1)}, f32[8,64,256]{2,1,0:T(8,128)S(1)}, u32[]{:S(2)}, u32[]{:S(2)}) collective-permute-start(f32[8,64,256]{2,1,0:T(8,128)S(1)} %get-tuple-element.41), channel_id=1, source_target_pairs={{0,16},{16,0},{32,48},{48,32},{64,80},{80,64},{96,112},{112,96},{1... | collective-permute-start | bytes 1572872 | tf_op jit(solution)/shard_map/ppermute | solution.py:306
  112.1 4.8 %collective-permute-start.8 = (f32[8,16,256]{2,1,0:T(8,128)S(1)}, f32[8,16,256]{2,1,0:T(8,128)S(1)}, u32[]{:S(2)}, u32[]{:S(2)}) collective-permute-start(f32[8,16,256]{2,1,0:T(8,128)S(1)} %get-tuple-element.50), channel_id=1, source_target_pairs={{0,15},{1,0},{2,1},{3,2},{4,3},{5,4},{6,5},{7,6},{8,7},{9,8},{10,9... | collective-permute-start | bytes 393224 | tf_op jit(solution)/shard_map/ppermute | solution.py:340
  113.7 7.7 %collective-permute-start.7 = (f32[8,16,256]{2,1,0:T(8,128)S(1)}, f32[8,16,256]{2,1,0:T(8,128)S(1)}, u32[]{:S(2)}, u32[]{:S(2)}) collective-permute-start(f32[8,16,256]{2,1,0:T(8,128)S(1)} %get-tuple-element.51), channel_id=1, source_target_pairs={{0,1},{1,2},{2,3},{3,4},{4,5},{5,6},{6,7},{7,8},{8,9},{9,10},{10,1... | collective-permute-start | bytes 393224 | tf_op jit(solution)/shard_map/ppermute | solution.py:341
